TPU v7x, 512 devices: a whole 4x4x16 slice. The times are simulated.
512 devices in a mesh: rep: 32 (over z, core), shard: 16 (over y, x).
Axes of the slice: x: 4, y: 4, z: 16, core: 2. Of those that a mesh axis runs over, the one named last changes fastest.
Arguments:
- inputs: bfloat16 [32, 2048, 8192], P('rep', 'shard'), may hold values from -6 to 6
- target: bfloat16 [32, 2048, 512], P('rep', 'shard'), may hold values from -6 to 6
- weights: bfloat16 [32, 8192, 512], P('rep', 'shard'), may hold values from -0.0625 to 0.0625
- feedback: bfloat16 [32, 8192, 512], P('rep', 'shard'), may hold values from -6 to 6
- counts: int32 [32, 16], P('rep', 'shard'), may hold values from 16 to 128, as said below
- blocks: int32 [32, 16, 128], P('rep', 'shard'), may hold values from 0 to 2047, as said below
Outputs:
- outer_update: float32 [8192, 512], P('shard')
- new_feedback: bfloat16 [32, 8192, 512], P('rep', 'shard')
Inputs may be any that keep to these rules, and one draw needn't show every extreme that they name: `counts`: in every shard index some replica keeps exactly 128 blocks. The 128 slots of one device hold distinct block numbers; only the first counts slots are kept; the others hold block numbers that this device does not keep (other replicas may keep them). All replicas of one shard index draw all their slots from a common set of 512 blocks.
All inputs are finite; a program needn't handle non-finite values.
Results may differ from a plain program's by a relative error of at most 0.0034.
Values may be sent and summed in bfloat16 or wider, within the bound.
A program may use at most 64 MiB of HBM per device.

v0:
```python
import jax
import jax.numpy as jnp
from jax import lax
from jax.sharding import PartitionSpec as P


def on_device(inputs, target, weights, feedback, counts, blocks):
    tokens = inputs[0]
    rows_w = weights[0]
    tok_dev = tokens.shape[0]
    n_rep = lax.axis_size("rep")
    columns = lax.all_to_all(tokens, "shard", split_axis=1, concat_axis=0, tiled=True)
    window = tokens
    key_proj = jnp.dot(
        window,
        lax.all_gather(rows_w, "shard", axis=0, tiled=True),
        preferred_element_type=jnp.float32,
    )
    slopes = ((key_proj - target[0].astype(jnp.float32)) / tok_dev).astype(jnp.bfloat16)
    window = columns
    gradient = lax.dot_general(
        window,
        lax.all_gather(slopes, "shard", axis=0, tiled=True),
        (((0,), (0,)), ((), ())),
        preferred_element_type=jnp.float32,
    )
    pseudo = gradient + feedback[0].astype(jnp.float32)
    flattened = pseudo.reshape(-1, 128)
    n_blocks = flattened.shape[0]
    slot_list = blocks[0, 0]
    slot_total = slot_list.shape[0]
    in_use = (jnp.arange(slot_total, dtype=jnp.int32) < counts[0, 0]).astype(jnp.float32)
    chosen_values = flattened[slot_list] * in_use[:, None]
    kept_mask = jnp.zeros((n_blocks,), jnp.float32).at[slot_list].add(in_use)
    residue = jnp.where(kept_mask[:, None] > 0, jnp.zeros_like(flattened), flattened)
    new_feedback = residue.reshape(rows_w.shape).astype(jnp.bfloat16)
    all_values, all_slots = (
        lax.all_gather(chosen_values, "rep", axis=0, tiled=True),
        lax.all_gather(slot_list.astype(jnp.float32), "rep", axis=0, tiled=True),
    )
    summed = jnp.zeros((n_blocks, 128), jnp.float32).at[all_slots.astype(jnp.int32)].add(all_values)
    outer_update = (summed / n_rep).reshape(rows_w.shape)
    return (outer_update, new_feedback[None])


def solution(mesh):
    placed = (
        P("rep", "shard", None),
        P("rep", "shard", None),
        P("rep", "shard", None),
        P("rep", "shard", None),
        P("rep", "shard"),
        P("rep", "shard", None),
    )
    return jax.shard_map(
        on_device,
        mesh=mesh,
        in_specs=placed,
        out_specs=(P("shard", None), P("rep", "shard", None)),
        check_vma=False,
    )
```

profile of v0, /device:TPU:1, one launch (start us, length us, event | category | flops | bytes accessed | tf_op | source)
XLA Modules:
  0.0 286.8 jit_solution(17193459561420966818)
XLA Ops:
  7.2 0.7 all-gather.10.cloned.1.call-update
  8.0 94.5 %all-gather.10.cloned.1.call-done = bf16[1,8192,512]{2,1,0:T(8,128)(2,1)} async-done(((bf16[1,512,512]{2,1,0:T(8,128)(2,1)}), bf16[1,8192,512]{2,1,0:T(8,128)(2,1)}) %all-gather.10.cloned.1.call-update) | async-done | bytes 8388624 | tf_op jit(solution)/shard_map/all_gather | solution.py:16
  102.4 5.9 %fusion.14 = bf16[128,512]{1,0:T(8,128)(2,1)} fusion(bf16[1,8192,512]{2,1,0:T(8,128)(2,1)} %all-gather.10.cloned.1.call-done, bf16[1,128,8192]{2,1,0:T(8,128)(2,1)} %param.6, bf16[1,128,512]{2,1,0:T(8,128)(2,1)} %param.7), kind=kOutput, calls=%fused_computation.10 | convolution fusion | flops 1074003968 | bytes 10747904 | tf_op jit(solution)/shard_map/dot_general | solution.py:14
  108.3 2.4 copy.14
  110.8 5.1 %all-to-all-start = ((bf16[128,16,512]{0,2,1:T(8,128)(2,1)}), bf16[128,16,512]{0,2,1:T(8,128)(2,1)S(1)}, u32[]{:S(2)}, u32[]{:S(2)}) async-start(bf16[128,16,512]{0,2,1:T(8,128)(2,1)} %bitcast.44), calls=%async_computation | async-start | bytes 4194304 | tf_op jit(solution)/shard_map/all_to_all | solution.py:12
  115.9 0.0 all-gather.8.cloned.1.call-start
  116.6 1.3 scatter_custom_fusion.1
  117.9 0.3 broadcast_in_dim.27
  118.2 0.1 copy.18
  118.3 0.2 copy.16
  118.6 29.5 %all-to-all-done = bf16[128,16,512]{0,2,1:T(8,128)(2,1)S(1)} async-done(((bf16[128,16,512]{0,2,1:T(8,128)(2,1)}), bf16[128,16,512]{0,2,1:T(8,128)(2,1)S(1)}, u32[]{:S(2)}, u32[]{:S(2)}) %all-to-all-start) | async-done | bytes 2097184 | tf_op jit(solution)/shard_map/all_to_all | solution.py:12
  148.0 2.6 copy.15
  150.6 27.6 %all-gather.6.cloned.1.call-done = bf16[2048,512]{1,0:T(8,128)(2,1)} async-done(((bf16[128,512]{1,0:T(8,128)(2,1)}), bf16[2048,512]{1,0:T(8,128)(2,1)}) %all-gather.6.cloned.1.call-update) | async-done | bytes 2097168 | tf_op jit(solution)/shard_map/all_gather | solution.py:23
  178.2 3.5 %select_convert_fusion = (bf16[512,512]{0,1:T(8,128)(2,1)S(1)}, f32[512,512]{0,1:T(8,128)S(1)}) fusion(pred[512,4]{0,1:T(4,128)(4,1)S(1)} %copy.18, bf16[1,512,512]{1,2,0:T(8,128)(2,1)S(1)} %copy.16, bf16[2048,512]{1,0:T(8,128)(2,1)} %all-gather.6.cloned.1.call-done, bf16[2048,512]{1,0:T(8,128)(2,1)} %bitcast.45), kind=kOutput, calls=%fused_computation.11 | convolution fusion | flops 1074528256 | bytes 6293504 | tf_op jit(solution)/shard_map/dot_general | solution.py:21
  181.7 0.3 copy.17
  182.1 0.1 reshape.58
  182.2 0.6 gather_fusion
  182.8 0.7 broadcast_multiply_fusion.1
  183.5 32.1 %all-gather = f32[1,1,4096]{2,1,0:T(1,128)S(1)} all-gather(f32[1,1,128]{2,1,0:T(1,128)S(1)} %convert_element_type.34), channel_id=2, replica_groups=mesh['rep'=32,'shard'=16] {'rep'}, dimensions={2}, use_global_device_ids=true | all-gather | bytes 16896 | tf_op jit(solution)/shard_map/all_gather | solution.py:39
  215.7 1.0 copy.19
  216.7 39.5 %all-gather.8.cloned.1.call-done = f32[4096,128]{1,0:T(8,128)} async-done(((f32[128,128]{1,0:T(8,128)}), f32[4096,128]{1,0:T(8,128)}) %all-gather.8.cloned.1.call-update) | async-done | bytes 2097168 | tf_op jit(solution)/shard_map/all_gather | solution.py:38
  256.2 22.9 %scatter_custom_fusion = f32[2048,128]{1,0:T(8,128)S(1)} fusion(s32[4096]{0:T(1024)S(1)} %compare_select_fusion, f32[4096,128]{1,0:T(8,128)} %all-gather.8.cloned.1.call-done, f32[]{:T(128)} %constant.5.clone.1), kind=kCustom, calls=%fused_computation.13 | custom fusion | flops 524288 | bytes 1049088 | tf_op jit(solution)/shard_map/scatter-add | solution.py:41
  279.1 0.1 broadcast_multiply_fusion
  279.2 1.1 reshape.59
  (17 shorter events, 0.2 us)
Async XLA Ops:
  7.2 95.2 %all-gather.10.cloned.1.call-start = ((), (), s32[]{:S(2)}) async-start(), calls=%async_computation.3 | async-start | bytes 8912896 | tf_op jit(solution)/shard_map/all_gather | solution.py:16
  7.9 100.4 %copy-start = (bf16[1,128,8192]{2,1,0:T(8,128)(2,1)S(1)}, bf16[1,128,8192]{2,1,0:T(8,128)(2,1)}, u32[]{:S(2)}) copy-start(bf16[1,128,8192]{2,1,0:T(8,128)(2,1)} %param.6) | copy-start | bytes 6291460
  7.9 170.3 %all-gather.6.cloned.1.call-start = ((), (), s32[]{:S(2)}) async-start(), calls=%async_computation.1 | async-start | bytes 2228224 | tf_op jit(solution)/shard_map/all_gather | solution.py:23
  110.8 5.8 %copy-start.2 = (s32[1,1,128]{2,1,0:T(1,128)S(1)}, s32[1,1,128]{2,1,0:T(1,128)}, u32[]{:S(2)}) copy-start(s32[1,1,128]{2,1,0:T(1,128)} %param.11) | copy-start | bytes 1540
  110.8 7.6 %copy-start.1 = (bf16[1,512,512]{2,1,0:T(8,128)(2,1)S(1)}, bf16[1,512,512]{2,1,0:T(8,128)(2,1)}, u32[]{:S(2)}) copy-start(bf16[1,512,512]{2,1,0:T(8,128)(2,1)} %param.9) | copy-start | bytes 1572868
  110.8 37.3 %all-to-all-start = ((bf16[128,16,512]{0,2,1:T(8,128)(2,1)}), bf16[128,16,512]{0,2,1:T(8,128)(2,1)S(1)}, u32[]{:S(2)}, u32[]{:S(2)}) async-start(bf16[128,16,512]{0,2,1:T(8,128)(2,1)} %bitcast.44), calls=%async_computation | async-start | bytes 4194304 | tf_op jit(solution)/shard_map/all_to_all | solution.py:12
  115.9 140.3 %all-gather.8.cloned.1.call-start = ((), (), s32[]{:S(2)}) async-start(), calls=%async_computation.2 | async-start | bytes 2162688 | tf_op jit(solution)/shard_map/all_gather | solution.py:38
Sparse Core Ops, SparseCore 0:
  11.0 91.3 all-gather.9
  108.4 69.7 all-gather.5
  183.7 72.4 all-gather.7
where the time goes:
time: 287 us
  waiting for transfers between devices  192 us (67%)
  blocking collectives  32.1 us (11%)
  other arithmetic  25 us (9%)
  between operations  14.5 us (5%)
  matrix products  9.39 us (3%)
  local copies, waits for them, and re-layouts  8.84 us (3%)
  starting transfers between devices  5.23 us (2%)
    all_gather x1, waiting for transfers between devices, on_device(): lax.all_gather(rows_w, 'shard', axis=0, tiled=True)  94.5 us
    all_gather x1, waiting for transfers between devices, on_device(): lax.all_gather(chosen_values, 'rep', axis=0, tiled=True)  39.5 us
    all_gather x1, blocking collectives, on_device(): lax.all_gather(slot_list.astype(jnp.float32), 'rep', axis=0, tiled=True)  32.1 us
    all_to_all x1, waiting for transfers between devices, on_device(): lax.all_to_all(tokens, 'shard', split_axis=1, concat_axis=0, tiled=True)  29.5 us
    all_gather x1, waiting for transfers between devices, on_device(): lax.all_gather(slopes, 'shard', axis=0, tiled=True)  27.6 us
    scatter-add x1, other arithmetic, on_device(): jnp.zeros((n_blocks, 128), jnp.float32).at[all_slots.astype(jnp.int32)]  22.9 us
    dot_general x1, matrix products, on_device(): jnp.dot(window, lax.all_gather(rows_w, 'shard', axis=0, tiled=True), pref...  5.9 us
  transfers between devices with their start and end apart: 4, of which 4 were waited for; matrix products, arithmetic and copies ran while one was open for 3% of the time, Pallas kernels for 0%

commit v1 on v0

v1 whole, which is shorter than its diff:
```python
import jax
import jax.numpy as jnp
from jax import lax
from jax.experimental import pallas as pl
from jax.experimental.pallas import tpu as pltpu
from jax.sharding import PartitionSpec as P

MESH = pl.DeviceIdType.MESH
F32, BF16, I32 = jnp.float32, jnp.bfloat16, jnp.int32
UNUSED = 1 << 16
FAR_FIRST = (2, 1, 3)


def dot(a, b):
    return jnp.dot(a, b, preferred_element_type=F32)


def dot_nt(a, b):
    return lax.dot_general(a, b, (((1,), (1,)), ((), ())), preferred_element_type=F32)


def kernel(
    x_ref, tgt_ref, w_ref, fb_ref, cnt_ref, slot_ref,
    outer_ref, newfb_ref,
    xs, xt, wg, acc, kp_out, kp_in, slopes, g_own, g_out, g_in, k_out, k_in, k_own,
    meta, meta_b, meta_z, sel, expand, pool, kept, pool_val, pool_in, part16, rs_in, res,
    x_send, x_recv, w_send, w_recv, loc_sem, kp_send, kp_recv, sl_send, sl_recv,
    g_send, g_recv, k_send, k_recv, m_send, m_recv, mz_send, mz_recv,
    p_send, p_recv, rs_send, rs_recv, ag_send, ag_recv, q_send, q_recv,
):
    rep, shard = lax.axis_index("rep"), lax.axis_index("shard")
    core, z = lax.rem(rep, 2), rep // 2
    y, x = shard // 4, lax.rem(shard, 4)
    a = x * (1 - core) + y * core
    b = y * (1 - core) + x * core

    def shard_of(aa, bb):
        return (bb * (1 - core) + aa * core) * 4 + (aa * (1 - core) + bb * core)

    def along_a(k):
        return (rep, shard_of(lax.rem(a + k, 4), b))

    def along_b(k):
        return (rep, shard_of(a, lax.rem(b + k, 4)))

    def along_z(k):
        return (lax.rem(rep + 2 * k, 32), shard)

    twin = (rep + 1 - 2 * core, shard)

    def remote(src, dst, send, recv, device):
        return pltpu.make_async_remote_copy(
            src_ref=src, dst_ref=dst, send_sem=send, recv_sem=recv, device_id=device, device_id_type=MESH
        )

    barrier = pltpu.get_barrier_semaphore()
    for k in (1, 2, 3):
        pl.semaphore_signal(barrier, inc=1, device_id=along_a(k), device_id_type=MESH)
        pl.semaphore_signal(barrier, inc=1, device_id=along_b(k), device_id_type=MESH)
    pl.semaphore_signal(barrier, inc=1, device_id=twin, device_id_type=MESH)

    @pl.loop(1, 16)
    def _(k):
        pl.semaphore_signal(barrier, inc=1, device_id=along_z(k), device_id_type=MESH)

    in_use = lax.broadcasted_iota(I32, (8, 128), 1) < cnt_ref[0, 0]
    meta[0] = jnp.where(in_use, jnp.broadcast_to(slot_ref[...], (8, 128)), UNUSED)
    pl.semaphore_wait(barrier, 22)

    m_copies = [remote(meta.at[0], meta_b.at[4 - k], m_send.at[k], m_recv.at[4 - k], along_b(k)) for k in (1, 2, 3)]
    m_copies.append(remote(meta.at[0], meta.at[1], m_send.at[0], m_recv.at[0], twin))
    for copy in m_copies:
        copy.start()
    locals_ = [pltpu.make_async_copy(w_ref, wg.at[0], loc_sem.at[4])]
    for j in range(4):
        own = pl.multiple_of(shard_of(a, lax.rem(b + j, 4)) * 512, 512)
        locals_.append(pltpu.make_async_copy(x_ref.at[:, pl.ds(own, 512)], xs.at[j, pl.ds(0, 128)], loc_sem.at[j]))
    x_copies, w_copies = {}, {}
    for k in FAR_FIRST:
        w_copies[k] = remote(w_ref, wg.at[4 - k], w_send.at[k], w_recv.at[4 - k], along_b(k))
        w_copies[k].start()
    for j in (0, 1, 3, 2):
        for k in FAR_FIRST:
            cols = pl.multiple_of(shard_of(lax.rem(a + k, 4), lax.rem(b + j, 4)) * 512, 512)
            x_copies[j, k] = remote(
                x_ref.at[:, pl.ds(cols, 512)], xs.at[j, pl.ds((4 - k) * 128, 128)],
                x_send.at[j, k], x_recv.at[j, 4 - k], along_a(k),
            )
            x_copies[j, k].start()
    for copy in locals_:
        copy.start()

    m_copies[3].wait()
    row0 = lax.broadcasted_iota(I32, (8, 128), 0) == 0
    meta_z[0] = jnp.where(row0, meta[0], meta[1])

    @pl.loop(1, 16)
    def _(k):
        remote(meta_z.at[0], meta_z.at[16 - k], mz_send.at[k], mz_recv.at[16 - k], along_z(k)).start()

    rows512 = lax.broadcasted_iota(I32, (512, 128), 0)
    rows128 = lax.broadcasted_iota(I32, (128, 128), 0)
    lanes128 = lax.broadcasted_iota(I32, (128, 128), 1)
    own_list = meta[0, 0:1, :]
    own_rows = jnp.where(rows512 == (own_list >> 2), 1.0, 0.0).astype(BF16)
    for c in range(4):
        is_c = jnp.where((jnp.broadcast_to(own_list, (128, 128)) & 3) == c, 1.0, 0.0).astype(BF16)
        kept[:, c * 128:(c + 1) * 128] = dot_nt(own_rows, is_c).astype(BF16)
    for k in (1, 2, 3):
        m_copies[k - 1].wait()
    for j in range(4):
        lst = meta[0, 0:1, :] if j == 0 else meta_b[j, 0:1, :]
        turned = jnp.transpose(jnp.broadcast_to(lst, (128, 128)))
        key = (turned & 3) * 512 + (turned >> 2)
        for n in range(16):
            sel[j, :, n * 128:(n + 1) * 128] = jnp.where(key == lanes128 + n * 128, 1.0, 0.0).astype(BF16)

    @pl.loop(1, 16)
    def _(k):
        remote(meta_z.at[0], meta_z.at[16 - k], mz_send.at[k], mz_recv.at[16 - k], along_z(k)).wait_send()
        remote(meta_z.at[0], meta_z.at[k], mz_send.at[k], mz_recv.at[k], along_z(k)).wait_recv()

    def count(i, total):
        for r in range(2):
            lst = meta_z[i, r:r + 1, :]
            in_rows = jnp.where(rows512 == (lst >> 2), 1.0, 0.0).astype(BF16)
            in_cols = jnp.where(rows128 == (jnp.broadcast_to(lst, (128, 128)) & 3), 1.0, 0.0).astype(BF16)
            total = total + dot_nt(in_rows, in_cols)
        return total

    present = lax.fori_loop(0, 16, count, jnp.zeros((512, 128), F32)) > 0.5
    lower = jnp.where(
        lax.broadcasted_iota(I32, (512, 512), 0) >= lax.broadcasted_iota(I32, (512, 512), 1), 1.0, 0.0
    ).astype(BF16)
    upto = dot(lower, jnp.where(present, 1.0, 0.0).astype(BF16))
    totals = upto[511:512, :]
    lane = lax.broadcasted_iota(I32, (1, 128), 1)
    offset = jnp.zeros((1, 128), F32)
    for c in range(3):
        offset = offset + jnp.where(lane > c, totals[:, c:c + 1], 0.0)
    rank = jnp.where(present, upto - 1.0 + offset, -1.0)
    places = lax.broadcasted_iota(I32, (512, 512), 1).astype(F32)
    for c in range(4):
        expand[c] = jnp.where(rank[:, c:c + 1] == places, 1.0, 0.0).astype(BF16)
    turned_rank = jnp.transpose(rank)[0:16, :]
    high = jnp.floor(turned_rank * (1.0 / 16.0))
    low = turned_rank - high * 16.0
    own_rank = dot(high.astype(BF16), own_rows) * 16.0 + dot(low.astype(BF16), own_rows)
    is_col = lax.broadcasted_iota(I32, (16, 128), 0) == (jnp.broadcast_to(own_list, (16, 128)) & 3)
    own_rank = jnp.sum(jnp.where(is_col, own_rank, 0.0), axis=0, keepdims=True)
    own_rank = jnp.where(own_list < UNUSED, own_rank, -1.0)
    pool[...] = jnp.where(rows512.astype(F32) == own_rank, 1.0, 0.0).astype(BF16)

    locals_[0].wait()
    for n, j in enumerate((0, 1, 3, 2)):
        locals_[1 + j].wait()
        if j:
            w_copies[4 - j].wait_recv()
        for k in FAR_FIRST:
            x_copies[j, 4 - k].wait_recv()
        part = dot(xs[j], wg[j])
        acc[...] = part if n == 0 else acc[...] + part
    kp_copies = {}
    for k in FAR_FIRST:
        kp_out[k] = acc[k * 128:(k + 1) * 128, :].astype(BF16)
        kp_copies[k] = remote(kp_out.at[k], kp_in.at[4 - k], kp_send.at[k], kp_recv.at[4 - k], along_a(k))
        kp_copies[k].start()
    for j in range(2):
        xt[j] = jnp.transpose(xs[j])
    for k in (1, 3, 2):
        kp_copies[4 - k].wait_recv()
    key_proj = acc[0:128, :]
    for k in (1, 2, 3):
        key_proj = key_proj + kp_in[k].astype(F32)
    slopes[0:128, :] = ((key_proj - tgt_ref[...].astype(F32)) * (1.0 / 128.0)).astype(BF16)
    sl_copies = {}
    for k in FAR_FIRST:
        sl_copies[k] = remote(
            slopes.at[pl.ds(0, 128)], slopes.at[pl.ds((4 - k) * 128, 128)],
            sl_send.at[k], sl_recv.at[4 - k], along_a(k),
        )
        sl_copies[k].start()
    for j in range(2, 4):
        xt[j] = jnp.transpose(xs[j])
    for k in (1, 3, 2):
        sl_copies[4 - k].wait_recv()

    k_copies, g_copies = {}, {}
    for j in (2, 1, 3, 0):
        part = dot(xt[j], slopes[...])
        if j == 0:
            g_own[...] = part
        g_out[j] = part.astype(BF16)
        blocks = jnp.zeros((128, 128), F32)
        for c in range(4):
            blocks = blocks + dot(sel[j, :, c * 512:(c + 1) * 512], g_out[j, :, c * 128:(c + 1) * 128])
        if j == 0:
            for c in range(4):
                blocks = blocks + dot(sel[0, :, c * 512:(c + 1) * 512], fb_ref[:, c * 128:(c + 1) * 128])
            k_own[...] = blocks
        else:
            k_out[j] = blocks.astype(BF16)
            k_copies[j] = remote(k_out.at[j], k_in.at[4 - j], k_send.at[j], k_recv.at[4 - j], along_b(j))
            k_copies[j].start()
    for j in FAR_FIRST:
        g_copies[j] = remote(g_out.at[j], g_in.at[4 - j], g_send.at[j], g_recv.at[4 - j], along_b(j))
        g_copies[j].start()

    for j in (1, 3, 2):
        k_copies[4 - j].wait_recv()
    values = k_own[...]
    for j in (1, 2, 3):
        values = values + k_in[j].astype(F32)
    top = values.astype(BF16)
    rest = (values - top.astype(F32)).astype(BF16)
    both = dot(pool[...], jnp.concatenate([top, rest], axis=1))
    pool_val[...] = both[:, :128] + both[:, 128:]
    mine = pl.multiple_of(core * 256, 256)
    other = pl.multiple_of((1 - core) * 256, 256)
    p_copy = remote(pool_val.at[pl.ds(other, 256)], pool_in, p_send, p_recv, twin)
    p_copy.start()
    p_copy.wait_recv()
    pool_in[...] = pool_in[...] + pool_val[pl.ds(mine, 256), :]
    part16[...] = pool_in[...].astype(BF16)

    @pl.loop(0, 15)
    def _(i):
        k = lax.rem(i + 8, 15) + 1
        to = pl.multiple_of(lax.rem(z + k, 16) * 16, 16)
        remote(part16.at[pl.ds(to, 16)], rs_in.at[16 - k], rs_send.at[k], rs_recv.at[16 - k], along_z(k)).start()

    @pl.loop(1, 16)
    def _(k):
        to = pl.multiple_of(lax.rem(z + k, 16) * 16, 16)
        remote(part16.at[pl.ds(to, 16)], rs_in.at[k], rs_send.at[k], rs_recv.at[k], along_z(k)).wait()

    total = pool_in[pl.ds(pl.multiple_of(z * 16, 16), 16), :]
    for k in range(1, 16):
        total = total + rs_in[k].astype(F32)
    here = pl.multiple_of(core * 256 + z * 16, 16)
    res[pl.ds(here, 16), :] = total * (1.0 / 32.0)

    @pl.loop(0, 15)
    def _(i):
        k = lax.rem(i + 8, 15) + 1
        remote(res.at[pl.ds(here, 16)], res.at[pl.ds(here, 16)], ag_send.at[k], ag_recv.at[16 - k], along_z(k)).start()

    for j in (1, 3, 2):
        g_copies[4 - j].wait_recv()
    whole = g_own[...] + fb_ref[...].astype(F32)
    for j in (1, 2, 3):
        whole = whole + g_in[j].astype(F32)
    newfb_ref[...] = jnp.where(kept[...].astype(F32) > 0.5, 0.0, whole).astype(BF16)

    @pl.loop(1, 16)
    def _(k):
        there = pl.multiple_of(core * 256 + lax.rem(z + k, 16) * 16, 16)
        remote(res.at[pl.ds(here, 16)], res.at[pl.ds(there, 16)], ag_send.at[k], ag_recv.at[k], along_z(k)).wait()

    q_copy = remote(res.at[pl.ds(mine, 256)], res.at[pl.ds(mine, 256)], q_send, q_recv, twin)
    q_copy.start()
    q_copy.wait()
    full = res[...]
    top = full.astype(BF16)
    rest = (full - top.astype(F32)).astype(BF16)
    pair = jnp.concatenate([top, rest], axis=1)
    for c in range(4):
        both = dot(expand[c], pair)
        outer_ref[:, c * 128:(c + 1) * 128] = both[:, :128] + both[:, 128:]

    for copies in (m_copies[:0], w_copies.values(), x_copies.values(), kp_copies.values(), sl_copies.values(),
                   k_copies.values(), g_copies.values()):
        for copy in copies:
            copy.wait_send()
    p_copy.wait_send()


def on_device(inputs, target, weights, feedback, counts, blocks):
    vmem = pl.BlockSpec(memory_space=pltpu.VMEM)
    hbm = pl.BlockSpec(memory_space=pl.ANY)
    sem = pltpu.SemaphoreType.DMA
    outer, newfb = pl.pallas_call(
        kernel,
        out_shape=(jax.ShapeDtypeStruct((512, 512), F32), jax.ShapeDtypeStruct((512, 512), BF16)),
        in_specs=[hbm, vmem, hbm, vmem, pl.BlockSpec(memory_space=pltpu.SMEM), vmem],
        out_specs=(vmem, vmem),
        scratch_shapes=[
            pltpu.VMEM((4, 512, 512), BF16),
            pltpu.VMEM((4, 512, 512), BF16),
            pltpu.VMEM((4, 512, 512), BF16),
            pltpu.VMEM((512, 512), F32),
            pltpu.VMEM((4, 128, 512), BF16),
            pltpu.VMEM((4, 128, 512), BF16),
            pltpu.VMEM((512, 512), BF16),
            pltpu.VMEM((512, 512), F32),
            pltpu.VMEM((4, 512, 512), BF16),
            pltpu.VMEM((4, 512, 512), BF16),
            pltpu.VMEM((4, 128, 128), BF16),
            pltpu.VMEM((4, 128, 128), BF16),
            pltpu.VMEM((128, 128), F32),
            pltpu.VMEM((2, 8, 128), I32),
            pltpu.VMEM((4, 8, 128), I32),
            pltpu.VMEM((16, 8, 128), I32),
            pltpu.VMEM((4, 128, 2048), BF16),
            pltpu.VMEM((4, 512, 512), BF16),
            pltpu.VMEM((512, 128), BF16),
            pltpu.VMEM((512, 512), BF16),
            pltpu.VMEM((512, 128), F32),
            pltpu.VMEM((256, 128), F32),
            pltpu.VMEM((256, 128), BF16),
            pltpu.VMEM((16, 16, 128), BF16),
            pltpu.VMEM((512, 128), F32),
            sem((4, 4)), sem((4, 4)), sem((4,)), sem((4,)), sem((5,)), sem((4,)), sem((4,)), sem((4,)), sem((4,)),
            sem((4,)), sem((4,)), sem((4,)), sem((4,)), sem((4,)), sem((4,)), sem((16,)), sem((16,)),
            sem, sem, sem((16,)), sem((16,)), sem((16,)), sem((16,)), sem, sem,
        ],
        compiler_params=pltpu.CompilerParams(
            collective_id=0, has_side_effects=True, vmem_limit_bytes=56 * 2**20
        ),
        name="outer_sync",
    )(inputs[0], target[0], weights[0], feedback[0], counts, blocks[0])
    return outer, newfb[None]


def solution(mesh):
    placed = (
        P("rep", "shard", None),
        P("rep", "shard", None),
        P("rep", "shard", None),
        P("rep", "shard", None),
        P("rep", "shard"),
        P("rep", "shard", None),
    )
    return jax.shard_map(
        on_device,
        mesh=mesh,
        in_specs=placed,
        out_specs=(P("shard", None), P("rep", "shard", None)),
        check_vma=False,
    )
```

time: 287 us -> 92.6 us (0.32)
  waiting for transfers between devices: 192 us -> 0 us
  Pallas kernels: 0 us -> 88 us
  blocking collectives: 32.1 us -> 0 us
  other arithmetic: 25 us -> 0 us
  between operations: 14.5 us -> 1.29 us
  matrix products: 9.39 us -> 0 us
  local copies, waits for them, and re-layouts: 8.84 us -> 3.12 us
  starting transfers between devices: 5.23 us -> 0 us
    all_gather x3 -> x0, waiting for transfers between devices: 162 us -> none  [the longest x1 94.5 us: on_device(): lax.all_gather(rows_w, 'shard', axis=0, tiled=True)]
    pallas_call x0 -> x1, Pallas kernels: none -> 88 us  [on_device(): pl.pallas_call(kernel, out_shape=(jax.ShapeDtypeStruct((512, 512), F32),...]
    all_gather x1 -> x0, blocking collectives: 32.1 us -> none  [on_device(): lax.all_gather(slot_list.astype(jnp.float32), 'rep', axis=0, tiled=True)]
    all_to_all x1 -> x0, waiting for transfers between devices: 29.5 us -> none  [on_device(): lax.all_to_all(tokens, 'shard', split_axis=1, concat_axis=0, tiled=True)]
    scatter-add x2 -> x0, other arithmetic: 24.2 us -> none  [the longest x1 22.9 us: on_device(): jnp.zeros((n_blocks, 128), jnp.float32).at[all_slots.astype(jnp.int32)]]
    dot_general x2 -> x0, matrix products: 9.39 us -> none  [the longest x1 5.9 us: on_device(): jnp.dot(window, lax.all_gather(rows_w, 'shard', axis=0, tiled=True), pref...]
    all_to_all x1 -> x0, starting transfers between devices: 5.11 us -> none  [on_device(): lax.all_to_all(tokens, 'shard', split_axis=1, concat_axis=0, tiled=True)]
  transfers between devices with their start and end apart: 4 -> 0, of which waited for: 4 -> 0; matrix products, arithmetic and copies ran while one was open for 3% -> 0% of each run, Pallas kernels for 0% -> 0%
where the time goes in v1:
time: 92.6 us; the launch traced here: 92.4 us
  Pallas kernels  88 us (95%)
  local copies, waits for them, and re-layouts  3.12 us (3%)
  between operations  1.29 us (1%)
    pallas_call x1, Pallas kernels, on_device(): pl.pallas_call(kernel, out_shape=(jax.ShapeDtypeStruct((512, 512), F32),...  88 us
    unnamed x4, local copies, waits for them, and re-layouts  3.12 us

profile of v1, /device:TPU:1, one launch (start us, length us, event | category | flops | bytes accessed | tf_op | source)
XLA Modules:
  0.0 92.4 jit_solution(6911819747447954512)
XLA Ops:
  1.3 88.0 %outer_sync.1 = (f32[512,512]{1,0:T(8,128)}, bf16[512,512]{1,0:T(8,128)(2,1)}) custom-call(bf16[128,8192]{1,0:T(8,128)(2,1)} %bitcast.6, bf16[128,512]{1,0:T(8,128)(2,1)} %bitcast.10, bf16[512,512]{1,0:T(8,128)(2,1)} %bitcast.8, bf16[512,512]{1,0:T(8,128)(2,1)} %bitcast.9, s32[1,1]{1,0:T(1,128)S(6)} %copy.10.cnt_ref, s32[1,128]{1,0:T(1,128)} %bitcast.11), custom_call_target="tpu_custom_call" | custom-call | tf_op jit(solution)/shard_map/outer_sync/pallas_call | solution.py:282
  89.3 0.0 copy-start
  89.3 2.3 %copy.11 = f32[512,512]{1,0:T(8,128)} copy(f32[512,512]{1,0:T(8,128)} %get-tuple-element.8) | data formatting | bytes 2097152
  91.6 0.0 copy-done
  91.6 0.8 copy.12
Async XLA Ops:
  89.3 2.3 %copy-start = (bf16[512,512]{1,0:T(8,128)(2,1)S(1)}, bf16[512,512]{1,0:T(8,128)(2,1)}, u32[]{:S(2)}) copy-start(bf16[512,512]{1,0:T(8,128)(2,1)} %get-tuple-element.5) | copy-start | bytes 1572868

commit v2 on v1

v2 whole, which is shorter than its diff:
```python
import jax
import jax.numpy as jnp
from jax import lax
from jax.experimental import pallas as pl
from jax.experimental.pallas import tpu as pltpu
from jax.sharding import PartitionSpec as P

MESH = pl.DeviceIdType.MESH
F32, BF16, I32 = jnp.float32, jnp.bfloat16, jnp.int32
UNUSED = 1 << 16
FAR_FIRST = (2, 1, 3)


def dot(a, b):
    return jnp.dot(a, b, preferred_element_type=F32)


def dot_nt(a, b):
    return lax.dot_general(a, b, (((1,), (1,)), ((), ())), preferred_element_type=F32)


def kernel(
    x_ref, tgt_ref, w_ref, fb_ref, cnt_ref, slot_ref,
    res_ref, rank_ref, newfb_ref,
    xs, xt, wg, acc, kp_out, kp_in, slopes, g_out, g_in, k_acc, k_out, k_in,
    meta, meta_b, meta_z, row_sel, col_of, x_sel, k_fb, pool, kept, pool_val, pool_in, part16, rs_in, res,
    tgt, fb, rank_out, newfb,
    x_send, x_recv, w_send, w_recv, loc_sem, kp_send, kp_recv, sl_send, sl_recv,
    g_send, g_recv, k_send, k_recv, m_send, m_recv, mz_send, mz_recv,
    p_send, p_recv, rs_send, rs_recv, ag_send, ag_recv, q_send, q_recv, out_sem, z_sem,
):
    rep, shard = lax.axis_index("rep"), lax.axis_index("shard")
    core, z = lax.rem(rep, 2), rep // 2
    y, x = shard // 4, lax.rem(shard, 4)
    a = x * (1 - core) + y * core
    b = y * (1 - core) + x * core

    def shard_of(aa, bb):
        return (bb * (1 - core) + aa * core) * 4 + (aa * (1 - core) + bb * core)

    def along_a(k):
        return (rep, shard_of(lax.rem(a + k, 4), b))

    def along_b(k):
        return (rep, shard_of(a, lax.rem(b + k, 4)))

    def along_z(k):
        return (lax.rem(rep + 2 * k, 32), shard)

    twin = (rep + 1 - 2 * core, shard)

    def remote(src, dst, send, recv, device):
        return pltpu.make_async_remote_copy(
            src_ref=src, dst_ref=dst, send_sem=send, recv_sem=recv, device_id=device, device_id_type=MESH
        )

    def far_first(i):
        return 8 + ((i + 1) // 2) * (1 - 2 * lax.rem(i + 1, 2))

    barrier = pltpu.get_barrier_semaphore()
    for k in (1, 2, 3):
        pl.semaphore_signal(barrier, inc=1, device_id=along_a(k), device_id_type=MESH)
        pl.semaphore_signal(barrier, inc=1, device_id=along_b(k), device_id_type=MESH)
    for device in (twin, along_z(1), along_z(15)):
        pl.semaphore_signal(barrier, inc=1, device_id=device, device_id_type=MESH)

    locals_ = []
    for j in range(4):
        own = pl.multiple_of(shard_of(a, lax.rem(b + j, 4)) * 512, 512)
        locals_.append(pltpu.make_async_copy(x_ref.at[:, pl.ds(own, 512)], xs.at[j, pl.ds(0, 128)], loc_sem.at[j]))
    locals_.append(pltpu.make_async_copy(w_ref, wg.at[0], loc_sem.at[4]))
    locals_.append(pltpu.make_async_copy(tgt_ref, tgt, loc_sem.at[5]))
    locals_.append(pltpu.make_async_copy(fb_ref, fb, loc_sem.at[6]))
    for copy in locals_:
        copy.start()
    in_use = lax.broadcasted_iota(I32, (8, 128), 1) < jnp.broadcast_to(cnt_ref[...], (8, 128))
    meta[0] = jnp.where(in_use, jnp.broadcast_to(slot_ref[...], (8, 128)), UNUSED)
    pl.semaphore_wait(barrier, 9)

    m_copies = [remote(meta.at[0], meta_b.at[4 - k], m_send.at[k], m_recv.at[4 - k], along_b(k)) for k in (1, 2, 3)]
    m_copies.append(remote(meta.at[0], meta.at[1], m_send.at[0], m_recv.at[0], twin))
    for copy in m_copies:
        copy.start()
    halves = (pl.ds(0, 256), pl.ds(256, 256))
    x_copies, w_copies = {}, {}
    for k, h in ((1, 0), (3, 1), (1, 1), (3, 0)):
        w_copies[k, h] = remote(
            w_ref.at[halves[h]], wg.at[4 - k, halves[h]], w_send.at[k, h], w_recv.at[4 - k, h], along_b(k)
        )
        w_copies[k, h].start()
    for j in (0, 1, 3, 2):
        for k in FAR_FIRST:
            cols = pl.multiple_of(shard_of(lax.rem(a + k, 4), lax.rem(b + j, 4)) * 512, 512)
            x_copies[j, k] = remote(
                x_ref.at[:, pl.ds(cols, 512)], xs.at[j, pl.ds((4 - k) * 128, 128)],
                x_send.at[j, k], x_recv.at[j, 4 - k], along_a(k),
            )
            x_copies[j, k].start()

    for n, step in enumerate((1, 2, 4)):
        for k in (step, 16 - step):
            pl.semaphore_signal(z_sem.at[n], inc=1, device_id=along_z(k), device_id_type=MESH)
        if step < 4:
            pl.semaphore_wait(z_sem.at[n], 2)
    for k, h in ((1, 0), (3, 1)):
        w_copies[k, h].wait_recv()
        w_copies[2, h] = remote(
            wg.at[4 - k, halves[h]], wg.at[2, halves[h]], w_send.at[2, h], w_recv.at[2, h], along_b(k)
        )
        w_copies[2, h].start()
    pl.semaphore_wait(z_sem.at[2], 2)
    m_copies[3].wait()
    row0 = lax.broadcasted_iota(I32, (8, 128), 0) == 0
    meta_z[0] = jnp.where(row0, meta[0], meta[1])

    @pl.loop(1, 16)
    def _(k):
        remote(meta_z.at[0], meta_z.at[16 - k], mz_send.at[k], mz_recv.at[16 - k], along_z(k)).start()

    rows512 = lax.broadcasted_iota(I32, (512, 128), 0)
    lanes512 = lax.broadcasted_iota(I32, (128, 512), 1)
    own_list = meta[0, 0:1, :]
    own_rows = jnp.where(rows512 == (own_list >> 2), 1.0, 0.0).astype(BF16)
    for c in range(4):
        is_c = jnp.where((jnp.broadcast_to(own_list, (128, 128)) & 3) == c, 1.0, 0.0).astype(BF16)
        kept[:, c * 128:(c + 1) * 128] = dot_nt(own_rows, is_c).astype(BF16)
    for k in (1, 2, 3):
        m_copies[k - 1].wait()
    for j in range(4):
        lst = meta[0, 0:1, :] if j == 0 else meta_b[j, 0:1, :]
        turned = jnp.transpose(jnp.broadcast_to(lst, (128, 128)))
        col_of[j] = turned & 3
        row_sel[j] = jnp.where((turned >> 2)[:, 0:1] == lanes512, 1.0, 0.0).astype(BF16)

    def pick(j, part, columns):
        blocks = jnp.zeros((128, 128), F32)
        for n, c in enumerate(columns):
            blocks = blocks + jnp.where(col_of[j] == c, part[:, n * 128:(n + 1) * 128], 0.0)
        return blocks

    for copy in locals_[4:]:
        copy.wait()
    k_fb[...] = pick(0, dot(row_sel[0], fb[...]), range(4))

    def prepare(j):
        xt[j] = jnp.transpose(xs[j])
        x_sel[j * 128:(j + 1) * 128, :] = dot_nt(row_sel[j], xs[j]).astype(BF16)

    for j in (0, 1, 3):
        locals_[j].wait()
        if j == 1:
            w_copies[3, 0].wait_recv()
        elif j == 3:
            w_copies[1, 1].wait_recv()
        for k in FAR_FIRST:
            x_copies[j, 4 - k].wait_recv()
        if j == 0:
            acc[...] = dot(xs[j], wg[j])
        else:
            acc[...] += dot(xs[j], wg[j])
        prepare(j)

    locals_[2].wait()
    w_copies[2, 0].wait_recv()
    w_copies[2, 1].wait_recv()
    for k in FAR_FIRST:
        x_copies[2, 4 - k].wait_recv()
    kp_copies, sl_copies = {}, {}
    for q in range(2):
        cols = slice(q * 256, (q + 1) * 256)
        part = acc[:, cols] + dot(xs[2], wg[2, :, cols])
        acc[0:128, cols] = part[0:128, :]
        for k in FAR_FIRST:
            kp_out[k, q] = part[k * 128:(k + 1) * 128, :].astype(BF16)
            kp_copies[k, q] = remote(
                kp_out.at[k, q], kp_in.at[4 - k, q], kp_send.at[k, q], kp_recv.at[4 - k, q], along_a(k)
            )
            kp_copies[k, q].start()
    prepare(2)

    @pl.loop(1, 16)
    def _(k):
        remote(meta_z.at[0], meta_z.at[16 - k], mz_send.at[k], mz_recv.at[16 - k], along_z(k)).wait_send()
        remote(meta_z.at[0], meta_z.at[k], mz_send.at[k], mz_recv.at[k], along_z(k)).wait_recv()

    def count(i, total):
        lst = jnp.concatenate([meta_z[2 * i + n, r:r + 1, :] for n in (0, 1) for r in (0, 1)], axis=1)
        in_rows = jnp.where(lax.broadcasted_iota(I32, (512, 512), 0) == (lst >> 2), 1.0, 0.0).astype(BF16)
        columns = jnp.broadcast_to(lst, (128, 512)) & 3
        in_cols = jnp.where(lax.broadcasted_iota(I32, (128, 512), 0) == columns, 1.0, 0.0).astype(BF16)
        return total + dot_nt(in_rows, in_cols)

    present = lax.fori_loop(0, 8, count, jnp.zeros((512, 128), F32)) > 0.5
    lower = jnp.where(
        lax.broadcasted_iota(I32, (512, 512), 0) >= lax.broadcasted_iota(I32, (512, 512), 1), 1.0, 0.0
    ).astype(BF16)
    upto = dot(lower, jnp.where(present, 1.0, 0.0).astype(BF16))
    totals = upto[511:512, :]
    lane = lax.broadcasted_iota(I32, (1, 128), 1)
    offset = jnp.zeros((1, 128), F32)
    for c in range(3):
        offset = offset + jnp.where(lane > c, totals[:, c:c + 1], 0.0)
    rank = jnp.where(present, upto - 1.0 + offset, -1.0)
    rank_out[...] = rank
    rank_copy = pltpu.make_async_copy(rank_out, rank_ref, out_sem.at[0])
    rank_copy.start()
    turned_rank = jnp.transpose(rank)[0:16, :]
    high = jnp.floor(turned_rank * (1.0 / 16.0))
    low = turned_rank - high * 16.0
    own_rank = dot(high.astype(BF16), own_rows) * 16.0 + dot(low.astype(BF16), own_rows)
    is_col = lax.broadcasted_iota(I32, (16, 128), 0) == (jnp.broadcast_to(own_list, (16, 128)) & 3)
    own_rank = jnp.sum(jnp.where(is_col, own_rank, 0.0), axis=0, keepdims=True)
    own_rank = jnp.where(own_list < UNUSED, own_rank, -1.0)
    pool[...] = jnp.where(rows512.astype(F32) == own_rank, 1.0, 0.0).astype(BF16)

    for q in range(2):
        cols = slice(q * 256, (q + 1) * 256)
        for k in (1, 3, 2):
            kp_copies[4 - k, q].wait_recv()
        key_proj = acc[0:128, cols]
        for k in (1, 2, 3):
            key_proj = key_proj + kp_in[k, q].astype(F32)
        slopes[q, 0:128, :] = ((key_proj - tgt[:, cols].astype(F32)) * (1.0 / 128.0)).astype(BF16)
        for k in FAR_FIRST:
            sl_copies[k, q] = remote(
                slopes.at[q, pl.ds(0, 128)], slopes.at[q, pl.ds((4 - k) * 128, 128)],
                sl_send.at[k, q], sl_recv.at[4 - k, q], along_a(k),
            )
            sl_copies[k, q].start()

    k_copies, g_copies = {}, {}
    for q in range(2):
        for k in (1, 3, 2):
            sl_copies[4 - k, q].wait_recv()
        part = dot(x_sel[...], slopes[q])
        for j in (2, 1, 3, 0):
            blocks = pick(j, part[j * 128:(j + 1) * 128, :], (2 * q, 2 * q + 1))
            if q == 0:
                k_acc[j] = blocks
            elif j == 0:
                k_acc[0] = k_acc[0] + blocks + k_fb[...]
            else:
                k_out[j] = (k_acc[j] + blocks).astype(BF16)
                k_copies[j] = remote(k_out.at[j], k_in.at[4 - j], k_send.at[j], k_recv.at[4 - j], along_b(j))
                k_copies[j].start()
    for q in range(2):
        for j in FAR_FIRST:
            g_out[j, q] = dot(xt[j], slopes[q]).astype(BF16)
            g_copies[j, q] = remote(
                g_out.at[j, q], g_in.at[4 - j, q], g_send.at[j, q], g_recv.at[4 - j, q], along_b(j)
            )
            g_copies[j, q].start()

    for j in (1, 3, 2):
        k_copies[4 - j].wait_recv()
    values = k_acc[0]
    for j in (1, 2, 3):
        values = values + k_in[j].astype(F32)
    top = values.astype(BF16)
    rest = (values - top.astype(F32)).astype(BF16)
    both = dot(pool[...], jnp.concatenate([top, rest], axis=1))
    pool_val[...] = both[:, :128] + both[:, 128:]
    mine = pl.multiple_of(core * 256, 256)
    other = pl.multiple_of((1 - core) * 256, 256)
    p_copy = remote(pool_val.at[pl.ds(other, 256)], pool_in, p_send, p_recv, twin)
    p_copy.start()
    p_copy.wait_recv()
    pool_in[...] = pool_in[...] + pool_val[pl.ds(mine, 256), :]
    part16[...] = pool_in[...].astype(BF16)

    @pl.loop(0, 15)
    def _(i):
        k = far_first(i)
        to = pl.multiple_of(lax.rem(z + k, 16) * 16, 16)
        remote(part16.at[pl.ds(to, 16)], rs_in.at[16 - k], rs_send.at[k], rs_recv.at[16 - k], along_z(k)).start()

    @pl.loop(1, 16)
    def _(k):
        to = pl.multiple_of(lax.rem(z + k, 16) * 16, 16)
        remote(part16.at[pl.ds(to, 16)], rs_in.at[k], rs_send.at[k], rs_recv.at[k], along_z(k)).wait()

    here = pl.multiple_of(z * 16, 16)
    total = pool_in[pl.ds(here, 16), :]
    for k in range(1, 16):
        total = total + rs_in[k].astype(F32)
    res[pl.ds(here, 16), :] = (total * (1.0 / 32.0)).astype(BF16)

    @pl.loop(0, 15)
    def _(i):
        k = far_first(i)
        remote(res.at[pl.ds(here, 16)], res.at[pl.ds(here, 16)], ag_send.at[k], ag_recv.at[16 - k], along_z(k)).start()

    for q in range(2):
        cols = slice(q * 256, (q + 1) * 256)
        whole = dot(xt[0], slopes[q]) + fb[:, cols].astype(F32)
        for j in (1, 3, 2):
            g_copies[4 - j, q].wait_recv()
        for j in (1, 2, 3):
            whole = whole + g_in[j, q].astype(F32)
        newfb[:, cols] = jnp.where(kept[:, cols].astype(F32) > 0.5, 0.0, whole).astype(BF16)
    newfb_copy = pltpu.make_async_copy(newfb, newfb_ref, out_sem.at[1])
    newfb_copy.start()
    for copies in (w_copies, x_copies, kp_copies, sl_copies, k_copies, g_copies):
        for copy in copies.values():
            copy.wait_send()
    p_copy.wait_send()
    rank_copy.wait()

    @pl.loop(1, 16)
    def _(k):
        there = pl.multiple_of(lax.rem(z + k, 16) * 16, 16)
        remote(res.at[pl.ds(here, 16)], res.at[pl.ds(there, 16)], ag_send.at[k], ag_recv.at[k], along_z(k)).wait()

    q_copy = remote(res, res_ref.at[pl.ds(mine, 256)], q_send, q_recv, twin)
    q_copy.start()
    res_copy = pltpu.make_async_copy(res, res_ref.at[pl.ds(mine, 256)], out_sem.at[2])
    res_copy.start()
    newfb_copy.wait()
    res_copy.wait()
    q_copy.wait()


def expand(res_ref, rank_ref, newfb_ref, outer_ref, newfb_out_ref, res, rank, newfb, outer, sems):
    res_copy = pltpu.make_async_copy(res_ref, res, sems.at[0])
    rank_copy = pltpu.make_async_copy(rank_ref, rank, sems.at[1])
    newfb_copy = pltpu.make_async_copy(newfb_ref, newfb, sems.at[2])
    newfb_out_copy = pltpu.make_async_copy(newfb, newfb_out_ref, sems.at[7])
    rank_copy.start()
    res_copy.start()
    newfb_copy.start()
    rank_copy.wait()
    res_copy.wait()
    places = lax.broadcasted_iota(I32, (128, 512), 1).astype(F32)
    copies = []
    for r in range(4):
        rows = slice(r * 128, (r + 1) * 128)
        if r == 1:
            newfb_copy.wait()
            newfb_out_copy.start()
        for c in range(4):
            one_hot = jnp.where(rank[rows, c:c + 1] == places, 1.0, 0.0).astype(BF16)
            outer[rows, c * 128:(c + 1) * 128] = dot(one_hot, res[...])
        copies.append(pltpu.make_async_copy(
            outer.at[pl.ds(r * 128, 128)], outer_ref.at[pl.ds(r * 128, 128)], sems.at[3 + r]
        ))
        copies[r].start()
    for copy in copies:
        copy.wait()
    newfb_out_copy.wait()


def on_device(inputs, target, weights, feedback, counts, blocks):
    vmem = pl.BlockSpec(memory_space=pltpu.VMEM)
    hbm = pl.BlockSpec(memory_space=pl.ANY)
    sem = pltpu.SemaphoreType.DMA
    res, rank, newfb = pl.pallas_call(
        kernel,
        out_shape=(
            jax.ShapeDtypeStruct((512, 128), BF16),
            jax.ShapeDtypeStruct((512, 128), F32),
            jax.ShapeDtypeStruct((512, 512), BF16),
        ),
        in_specs=[hbm, hbm, hbm, hbm, vmem, vmem],
        out_specs=(hbm, hbm, hbm),
        scratch_shapes=[
            pltpu.VMEM((4, 512, 512), BF16),
            pltpu.VMEM((4, 512, 512), BF16),
            pltpu.VMEM((4, 512, 512), BF16),
            pltpu.VMEM((512, 512), F32),
            pltpu.VMEM((4, 2, 128, 256), BF16),
            pltpu.VMEM((4, 2, 128, 256), BF16),
            pltpu.VMEM((2, 512, 256), BF16),
            pltpu.VMEM((4, 2, 512, 256), BF16),
            pltpu.VMEM((4, 2, 512, 256), BF16),
            pltpu.VMEM((4, 128, 128), F32),
            pltpu.VMEM((4, 128, 128), BF16),
            pltpu.VMEM((4, 128, 128), BF16),
            pltpu.VMEM((2, 8, 128), I32),
            pltpu.VMEM((4, 8, 128), I32),
            pltpu.VMEM((16, 8, 128), I32),
            pltpu.VMEM((4, 128, 512), BF16),
            pltpu.VMEM((4, 128, 128), I32),
            pltpu.VMEM((512, 512), BF16),
            pltpu.VMEM((128, 128), F32),
            pltpu.VMEM((512, 128), BF16),
            pltpu.VMEM((512, 512), BF16),
            pltpu.VMEM((512, 128), F32),
            pltpu.VMEM((256, 128), F32),
            pltpu.VMEM((256, 128), BF16),
            pltpu.VMEM((16, 16, 128), BF16),
            pltpu.VMEM((256, 128), BF16),
            pltpu.VMEM((128, 512), BF16),
            pltpu.VMEM((512, 512), BF16),
            pltpu.VMEM((512, 128), F32),
            pltpu.VMEM((512, 512), BF16),
            sem((4, 4)), sem((4, 4)),
            sem((4, 2)), sem((4, 2)),
            sem((7,)),
            sem((4, 2)), sem((4, 2)),
            sem((4, 2)), sem((4, 2)),
            sem((4, 2)), sem((4, 2)),
            sem((4,)), sem((4,)),
            sem((4,)), sem((4,)),
            sem((16,)), sem((16,)),
            sem, sem,
            sem((16,)), sem((16,)),
            sem((16,)), sem((16,)),
            sem, sem,
            sem((3,)),
            pltpu.SemaphoreType.REGULAR((3,)),
        ],
        compiler_params=pltpu.CompilerParams(
            collective_id=0, has_side_effects=True, vmem_limit_bytes=56 * 2**20
        ),
        name="outer_sync",
    )(inputs[0], target[0], weights[0], feedback[0], counts, blocks[0])
    outer, newfb = pl.pallas_call(
        expand,
        out_shape=(jax.ShapeDtypeStruct((512, 512), F32), jax.ShapeDtypeStruct((512, 512), BF16)),
        in_specs=[hbm, hbm, hbm],
        out_specs=(hbm, hbm),
        scratch_shapes=[
            pltpu.VMEM((512, 128), BF16), pltpu.VMEM((512, 128), F32), pltpu.VMEM((512, 512), BF16),
            pltpu.VMEM((512, 512), F32), sem((8,)),
        ],
        compiler_params=pltpu.CompilerParams(vmem_limit_bytes=56 * 2**20),
        name="expand_pool",
    )(res, rank, newfb)
    return outer, newfb[None]


def solution(mesh):
    placed = (
        P("rep", "shard", None),
        P("rep", "shard", None),
        P("rep", "shard", None),
        P("rep", "shard", None),
        P("rep", "shard"),
        P("rep", "shard", None),
    )
    return jax.shard_map(
        on_device,
        mesh=mesh,
        in_specs=placed,
        out_specs=(P("shard", None), P("rep", "shard", None)),
        check_vma=False,
    )
```

time: 92.6 us -> 74.9 us (0.81)
  Pallas kernels: 88 us -> 72.9 us
  local copies, waits for them, and re-layouts: 3.12 us -> 0 us
    pallas_call x1 -> x2, Pallas kernels: 88 us -> 72.9 us  [the longest x1 70.2 us: on_device(): pl.pallas_call(kernel, out_shape=(jax.ShapeDtypeStruct((512, 128), BF16),...]
    unnamed x4 -> x0, local copies, waits for them, and re-layouts: 3.12 us -> none
where the time goes in v2:
time: 74.9 us; the launch traced here: 74.2 us
  Pallas kernels  72.9 us (97%)
  between operations  1.29 us (2%)
    pallas_call x1, Pallas kernels, on_device(): pl.pallas_call(kernel, out_shape=(jax.ShapeDtypeStruct((512, 128), BF16),...  70.2 us
    pallas_call x1, Pallas kernels, on_device(): pl.pallas_call(expand, out_shape=(jax.ShapeDtypeStruct((512, 512), F32),...  2.72 us

profile of v2, /device:TPU:1, one launch (start us, length us, event | category | flops | bytes accessed | tf_op | source)
XLA Modules:
  0.0 74.2 jit_solution(755355536867927933)
XLA Ops:
  1.3 70.2 %outer_sync.1 = (bf16[512,128]{1,0:T(8,128)(2,1)}, f32[512,128]{1,0:T(8,128)}, bf16[512,512]{1,0:T(8,128)(2,1)}) custom-call(bf16[128,8192]{1,0:T(8,128)(2,1)} %bitcast.6, bf16[128,512]{1,0:T(8,128)(2,1)} %bitcast.9, bf16[512,512]{1,0:T(8,128)(2,1)} %bitcast.7, bf16[512,512]{1,0:T(8,128)(2,1)} %bitcast.8, s32[1,1]{1,0:T(1,128)S(6)} %copy.8.cnt_ref, ...), custom_call_target="tpu_custom_call" | custom-call | tf_op jit(solution)/shard_map/outer_sync/pallas_call | solution.py:356
  71.5 2.7 %expand_pool.1 = (f32[512,512]{1,0:T(8,128)}, bf16[512,512]{1,0:T(8,128)(2,1)}) custom-call(bf16[512,128]{1,0:T(8,128)(2,1)} %get-tuple-element.7.res_ref, f32[512,128]{1,0:T(8,128)} %get-tuple-element.8.rank_ref, bf16[512,512]{1,0:T(8,128)(2,1)} %get-tuple-element.9.newfb_ref), custom_call_target="tpu_custom_call" | custom-call | tf_op jit(solution)/shard_map/expand_pool/pallas_call | solution.py:417

commit v3 on v2

--- a/solution.py
+++ b/solution.py
@@ -22,11 +22,11 @@
 def kernel(
     x_ref, tgt_ref, w_ref, fb_ref, cnt_ref, slot_ref,
     res_ref, rank_ref, newfb_ref,
-    xs, xt, wg, acc, kp_out, kp_in, slopes, g_out, g_in, k_acc, k_out, k_in,
+    xs, xt, wg, acc, kp_out, kp_in, slopes, g_own, g_out, g_in, k_acc, k_out, k_in,
     meta, meta_b, meta_z, row_sel, col_of, x_sel, k_fb, pool, kept, pool_val, pool_in, part16, rs_in, res,
-    tgt, fb, rank_out, newfb,
+    tgt, fb, slot, cnt, rank_out, newfb,
     x_send, x_recv, w_send, w_recv, loc_sem, kp_send, kp_recv, sl_send, sl_recv,
-    g_send, g_recv, k_send, k_recv, m_send, m_recv, mz_send, mz_recv,
+    g_send, g_recv, k_send, k_recv, m_send, m_recv, mt_send, mt_recv, mz_send, mz_recv,
     p_send, p_recv, rs_send, rs_recv, ag_send, ag_recv, q_send, q_recv, out_sem, z_sem,
 ):
     rep, shard = lax.axis_index("rep"), lax.axis_index("shard")
@@ -54,6 +54,12 @@
             src_ref=src, dst_ref=dst, send_sem=send, recv_sem=recv, device_id=device, device_id_type=MESH
         )
 
+    def sent(view, sem):
+        remote(view, view, sem, sem, twin).wait_send()
+
+    def arrived(view, sem):
+        remote(view, view, sem, sem, twin).wait_recv()
+
     def far_first(i):
         return 8 + ((i + 1) // 2) * (1 - 2 * lax.rem(i + 1, 2))
 
@@ -64,38 +70,43 @@
     for device in (twin, along_z(1), along_z(15)):
         pl.semaphore_signal(barrier, inc=1, device_id=device, device_id_type=MESH)
 
-    locals_ = []
+    lists = [
+        pltpu.make_async_copy(slot_ref, slot, loc_sem.at[4]), pltpu.make_async_copy(cnt_ref, cnt, loc_sem.at[5])
+    ]
+    for copy in lists:
+        copy.start()
     for j in range(4):
         own = pl.multiple_of(shard_of(a, lax.rem(b + j, 4)) * 512, 512)
-        locals_.append(pltpu.make_async_copy(x_ref.at[:, pl.ds(own, 512)], xs.at[j, pl.ds(0, 128)], loc_sem.at[j]))
-    locals_.append(pltpu.make_async_copy(w_ref, wg.at[0], loc_sem.at[4]))
-    locals_.append(pltpu.make_async_copy(tgt_ref, tgt, loc_sem.at[5]))
-    locals_.append(pltpu.make_async_copy(fb_ref, fb, loc_sem.at[6]))
+        pltpu.make_async_copy(x_ref.at[:, pl.ds(own, 512)], xs.at[j, pl.ds(0, 128)], loc_sem.at[0]).start()
+    own_tokens = xs.at[:, pl.ds(0, 128)]
+    locals_ = [
+        pltpu.make_async_copy(w_ref, wg.at[0], loc_sem.at[1]),
+        pltpu.make_async_copy(tgt_ref, tgt, loc_sem.at[2]),
+        pltpu.make_async_copy(fb_ref, fb, loc_sem.at[3]),
+    ]
     for copy in locals_:
         copy.start()
-    in_use = lax.broadcasted_iota(I32, (8, 128), 1) < jnp.broadcast_to(cnt_ref[...], (8, 128))
-    meta[0] = jnp.where(in_use, jnp.broadcast_to(slot_ref[...], (8, 128)), UNUSED)
+    for copy in lists:
+        copy.wait()
+    in_use = lax.broadcasted_iota(I32, (8, 128), 1) < jnp.broadcast_to(cnt[...], (8, 128))
+    meta[0] = jnp.where(in_use, jnp.broadcast_to(slot[...], (8, 128)), UNUSED)
     pl.semaphore_wait(barrier, 9)
 
-    m_copies = [remote(meta.at[0], meta_b.at[4 - k], m_send.at[k], m_recv.at[4 - k], along_b(k)) for k in (1, 2, 3)]
-    m_copies.append(remote(meta.at[0], meta.at[1], m_send.at[0], m_recv.at[0], twin))
-    for copy in m_copies:
-        copy.start()
+    for k in (1, 2, 3):
+        remote(meta.at[0], meta_b.at[4 - k], m_send, m_recv, along_b(k)).start()
+    m_copy = remote(meta.at[0], meta.at[1], mt_send, mt_recv, twin)
+    m_copy.start()
     halves = (pl.ds(0, 256), pl.ds(256, 256))
-    x_copies, w_copies = {}, {}
     for k, h in ((1, 0), (3, 1), (1, 1), (3, 0)):
-        w_copies[k, h] = remote(
-            w_ref.at[halves[h]], wg.at[4 - k, halves[h]], w_send.at[k, h], w_recv.at[4 - k, h], along_b(k)
-        )
-        w_copies[k, h].start()
+        remote(
+            w_ref.at[halves[h]], wg.at[4 - k, halves[h]], w_send, w_recv.at[4 - k, h], along_b(k)
+        ).start()
     for j in (0, 1, 3, 2):
         for k in FAR_FIRST:
             cols = pl.multiple_of(shard_of(lax.rem(a + k, 4), lax.rem(b + j, 4)) * 512, 512)
-            x_copies[j, k] = remote(
-                x_ref.at[:, pl.ds(cols, 512)], xs.at[j, pl.ds((4 - k) * 128, 128)],
-                x_send.at[j, k], x_recv.at[j, 4 - k], along_a(k),
-            )
-            x_copies[j, k].start()
+            remote(
+                x_ref.at[:, pl.ds(cols, 512)], xs.at[j, pl.ds((4 - k) * 128, 128)], x_send, x_recv.at[j], along_a(k)
+            ).start()
 
     for n, step in enumerate((1, 2, 4)):
         for k in (step, 16 - step):
@@ -103,19 +114,16 @@
         if step < 4:
             pl.semaphore_wait(z_sem.at[n], 2)
     for k, h in ((1, 0), (3, 1)):
-        w_copies[k, h].wait_recv()
-        w_copies[2, h] = remote(
-            wg.at[4 - k, halves[h]], wg.at[2, halves[h]], w_send.at[2, h], w_recv.at[2, h], along_b(k)
-        )
-        w_copies[2, h].start()
+        arrived(wg.at[4 - k, halves[h]], w_recv.at[4 - k, h])
+        remote(wg.at[4 - k, halves[h]], wg.at[2, halves[h]], w_send, w_recv.at[2, 0], along_b(k)).start()
     pl.semaphore_wait(z_sem.at[2], 2)
-    m_copies[3].wait()
+    m_copy.wait()
     row0 = lax.broadcasted_iota(I32, (8, 128), 0) == 0
     meta_z[0] = jnp.where(row0, meta[0], meta[1])
 
     @pl.loop(1, 16)
     def _(k):
-        remote(meta_z.at[0], meta_z.at[16 - k], mz_send.at[k], mz_recv.at[16 - k], along_z(k)).start()
+        remote(meta_z.at[0], meta_z.at[16 - k], mz_send, mz_recv, along_z(k)).start()
 
     rows512 = lax.broadcasted_iota(I32, (512, 128), 0)
     lanes512 = lax.broadcasted_iota(I32, (128, 512), 1)
@@ -124,8 +132,7 @@
     for c in range(4):
         is_c = jnp.where((jnp.broadcast_to(own_list, (128, 128)) & 3) == c, 1.0, 0.0).astype(BF16)
         kept[:, c * 128:(c + 1) * 128] = dot_nt(own_rows, is_c).astype(BF16)
-    for k in (1, 2, 3):
-        m_copies[k - 1].wait()
+    arrived(meta_b.at[pl.ds(1, 3)], m_recv)
     for j in range(4):
         lst = meta[0, 0:1, :] if j == 0 else meta_b[j, 0:1, :]
         turned = jnp.transpose(jnp.broadcast_to(lst, (128, 128)))
@@ -138,8 +145,9 @@
             blocks = blocks + jnp.where(col_of[j] == c, part[:, n * 128:(n + 1) * 128], 0.0)
         return blocks
 
-    for copy in locals_[4:]:
+    for copy in locals_:
         copy.wait()
+    pltpu.make_async_copy(own_tokens, own_tokens, loc_sem.at[0]).wait()
     k_fb[...] = pick(0, dot(row_sel[0], fb[...]), range(4))
 
     def prepare(j):
@@ -147,41 +155,18 @@
         x_sel[j * 128:(j + 1) * 128, :] = dot_nt(row_sel[j], xs[j]).astype(BF16)
 
     for j in (0, 1, 3):
-        locals_[j].wait()
         if j == 1:
-            w_copies[3, 0].wait_recv()
+            arrived(wg.at[1, halves[0]], w_recv.at[1, 0])
         elif j == 3:
-            w_copies[1, 1].wait_recv()
-        for k in FAR_FIRST:
-            x_copies[j, 4 - k].wait_recv()
+            arrived(wg.at[3, halves[1]], w_recv.at[3, 1])
+        arrived(xs.at[j, pl.ds(128, 384)], x_recv.at[j])
         if j == 0:
             acc[...] = dot(xs[j], wg[j])
         else:
             acc[...] += dot(xs[j], wg[j])
         prepare(j)
 
-    locals_[2].wait()
-    w_copies[2, 0].wait_recv()
-    w_copies[2, 1].wait_recv()
-    for k in FAR_FIRST:
-        x_copies[2, 4 - k].wait_recv()
-    kp_copies, sl_copies = {}, {}
-    for q in range(2):
-        cols = slice(q * 256, (q + 1) * 256)
-        part = acc[:, cols] + dot(xs[2], wg[2, :, cols])
-        acc[0:128, cols] = part[0:128, :]
-        for k in FAR_FIRST:
-            kp_out[k, q] = part[k * 128:(k + 1) * 128, :].astype(BF16)
-            kp_copies[k, q] = remote(
-                kp_out.at[k, q], kp_in.at[4 - k, q], kp_send.at[k, q], kp_recv.at[4 - k, q], along_a(k)
-            )
-            kp_copies[k, q].start()
-    prepare(2)
-
-    @pl.loop(1, 16)
-    def _(k):
-        remote(meta_z.at[0], meta_z.at[16 - k], mz_send.at[k], mz_recv.at[16 - k], along_z(k)).wait_send()
-        remote(meta_z.at[0], meta_z.at[k], mz_send.at[k], mz_recv.at[k], along_z(k)).wait_recv()
+    arrived(meta_z.at[pl.ds(1, 15)], mz_recv)
 
     def count(i, total):
         lst = jnp.concatenate([meta_z[2 * i + n, r:r + 1, :] for n in (0, 1) for r in (0, 1)], axis=1)
@@ -191,6 +176,17 @@
         return total + dot_nt(in_rows, in_cols)
 
     present = lax.fori_loop(0, 8, count, jnp.zeros((512, 128), F32)) > 0.5
+    arrived(wg.at[2], w_recv.at[2, 0])
+    arrived(xs.at[2, pl.ds(128, 384)], x_recv.at[2])
+    for q in range(2):
+        cols = slice(q * 256, (q + 1) * 256)
+        part = acc[:, cols] + dot(xs[2], wg[2, :, cols])
+        acc[0:128, cols] = part[0:128, :]
+        for k in FAR_FIRST:
+            kp_out[q, k] = part[k * 128:(k + 1) * 128, :].astype(BF16)
+            remote(kp_out.at[q, k], kp_in.at[q, 4 - k], kp_send, kp_recv.at[q], along_a(k)).start()
+    prepare(2)
+
     lower = jnp.where(
         lax.broadcasted_iota(I32, (512, 512), 0) >= lax.broadcasted_iota(I32, (512, 512), 1), 1.0, 0.0
     ).astype(BF16)
@@ -215,23 +211,18 @@
 
     for q in range(2):
         cols = slice(q * 256, (q + 1) * 256)
-        for k in (1, 3, 2):
-            kp_copies[4 - k, q].wait_recv()
+        arrived(kp_in.at[q, pl.ds(1, 3)], kp_recv.at[q])
         key_proj = acc[0:128, cols]
         for k in (1, 2, 3):
-            key_proj = key_proj + kp_in[k, q].astype(F32)
+            key_proj = key_proj + kp_in[q, k].astype(F32)
         slopes[q, 0:128, :] = ((key_proj - tgt[:, cols].astype(F32)) * (1.0 / 128.0)).astype(BF16)
         for k in FAR_FIRST:
-            sl_copies[k, q] = remote(
-                slopes.at[q, pl.ds(0, 128)], slopes.at[q, pl.ds((4 - k) * 128, 128)],
-                sl_send.at[k, q], sl_recv.at[4 - k, q], along_a(k),
-            )
-            sl_copies[k, q].start()
-
-    k_copies, g_copies = {}, {}
-    for q in range(2):
-        for k in (1, 3, 2):
-            sl_copies[4 - k, q].wait_recv()
+            remote(
+                slopes.at[q, pl.ds(0, 128)], slopes.at[q, pl.ds((4 - k) * 128, 128)], sl_send, sl_recv.at[q], along_a(k)
+            ).start()
+
+    for q in range(2):
+        arrived(slopes.at[q, pl.ds(128, 384)], sl_recv.at[q])
         part = dot(x_sel[...], slopes[q])
         for j in (2, 1, 3, 0):
             blocks = pick(j, part[j * 128:(j + 1) * 128, :], (2 * q, 2 * q + 1))
@@ -241,18 +232,12 @@
                 k_acc[0] = k_acc[0] + blocks + k_fb[...]
             else:
                 k_out[j] = (k_acc[j] + blocks).astype(BF16)
-                k_copies[j] = remote(k_out.at[j], k_in.at[4 - j], k_send.at[j], k_recv.at[4 - j], along_b(j))
-                k_copies[j].start()
+                remote(k_out.at[j], k_in.at[4 - j], k_send, k_recv, along_b(j)).start()
     for q in range(2):
         for j in FAR_FIRST:
-            g_out[j, q] = dot(xt[j], slopes[q]).astype(BF16)
-            g_copies[j, q] = remote(
-                g_out.at[j, q], g_in.at[4 - j, q], g_send.at[j, q], g_recv.at[4 - j, q], along_b(j)
-            )
-            g_copies[j, q].start()
-
-    for j in (1, 3, 2):
-        k_copies[4 - j].wait_recv()
+            g_out[q, j] = dot(xt[j], slopes[q]).astype(BF16)
+
+    arrived(k_in.at[pl.ds(1, 3)], k_recv)
     values = k_acc[0]
     for j in (1, 2, 3):
         values = values + k_in[j].astype(F32)
@@ -272,13 +257,16 @@
     def _(i):
         k = far_first(i)
         to = pl.multiple_of(lax.rem(z + k, 16) * 16, 16)
-        remote(part16.at[pl.ds(to, 16)], rs_in.at[16 - k], rs_send.at[k], rs_recv.at[16 - k], along_z(k)).start()
-
-    @pl.loop(1, 16)
-    def _(k):
-        to = pl.multiple_of(lax.rem(z + k, 16) * 16, 16)
-        remote(part16.at[pl.ds(to, 16)], rs_in.at[k], rs_send.at[k], rs_recv.at[k], along_z(k)).wait()
-
+        remote(part16.at[pl.ds(to, 16)], rs_in.at[16 - k], rs_send, rs_recv, along_z(k)).start()
+
+    for q in range(2):
+        for j in FAR_FIRST:
+            remote(g_out.at[q, j], g_in.at[q, 4 - j], g_send, g_recv.at[q], along_b(j)).start()
+
+    for q in range(2):
+        g_own[q] = dot(xt[0], slopes[q])
+
+    arrived(rs_in.at[pl.ds(1, 15)], rs_recv)
     here = pl.multiple_of(z * 16, 16)
     total = pool_in[pl.ds(here, 16), :]
     for k in range(1, 16):
@@ -288,36 +276,38 @@
     @pl.loop(0, 15)
     def _(i):
         k = far_first(i)
-        remote(res.at[pl.ds(here, 16)], res.at[pl.ds(here, 16)], ag_send.at[k], ag_recv.at[16 - k], along_z(k)).start()
-
-    for q in range(2):
-        cols = slice(q * 256, (q + 1) * 256)
-        whole = dot(xt[0], slopes[q]) + fb[:, cols].astype(F32)
-        for j in (1, 3, 2):
-            g_copies[4 - j, q].wait_recv()
-        for j in (1, 2, 3):
-            whole = whole + g_in[j, q].astype(F32)
-        newfb[:, cols] = jnp.where(kept[:, cols].astype(F32) > 0.5, 0.0, whole).astype(BF16)
-    newfb_copy = pltpu.make_async_copy(newfb, newfb_ref, out_sem.at[1])
-    newfb_copy.start()
-    for copies in (w_copies, x_copies, kp_copies, sl_copies, k_copies, g_copies):
-        for copy in copies.values():
-            copy.wait_send()
-    p_copy.wait_send()
-    rank_copy.wait()
-
-    @pl.loop(1, 16)
-    def _(k):
-        there = pl.multiple_of(lax.rem(z + k, 16) * 16, 16)
-        remote(res.at[pl.ds(here, 16)], res.at[pl.ds(there, 16)], ag_send.at[k], ag_recv.at[k], along_z(k)).wait()
-
+        remote(res.at[pl.ds(here, 16)], res.at[pl.ds(here, 16)], ag_send, ag_recv, along_z(k)).start()
+
+    arrived(res.at[pl.ds(0, 240)], ag_recv)
     q_copy = remote(res, res_ref.at[pl.ds(mine, 256)], q_send, q_recv, twin)
     q_copy.start()
     res_copy = pltpu.make_async_copy(res, res_ref.at[pl.ds(mine, 256)], out_sem.at[2])
     res_copy.start()
-    newfb_copy.wait()
+
+    for q in range(2):
+        cols = slice(q * 256, (q + 1) * 256)
+        whole = g_own[q] + fb[:, cols].astype(F32)
+        arrived(g_in.at[q, pl.ds(1, 3)], g_recv.at[q])
+        for j in (1, 2, 3):
+            whole = whole + g_in[q, j].astype(F32)
+        newfb[:, cols] = jnp.where(kept[:, cols].astype(F32) > 0.5, 0.0, whole).astype(BF16)
+    newfb_copy = pltpu.make_async_copy(newfb, newfb_ref, out_sem.at[1])
+    newfb_copy.start()
+    sent(xs.at[pl.ds(0, 3)], x_send)
+    sent(wg.at[pl.ds(0, 3)], w_send)
+    sent(meta_b.at[pl.ds(1, 3)], m_send)
+    sent(meta_z.at[pl.ds(1, 15)], mz_send)
+    sent(kp_in.at[:, pl.ds(1, 3)], kp_send)
+    sent(slopes.at[:, pl.ds(128, 384)], sl_send)
+    sent(k_in.at[pl.ds(1, 3)], k_send)
+    sent(g_in.at[:, pl.ds(1, 3)], g_send)
+    sent(rs_in.at[pl.ds(1, 15)], rs_send)
+    sent(res.at[pl.ds(0, 240)], ag_send)
+    p_copy.wait_send()
+    rank_copy.wait()
     res_copy.wait()
     q_copy.wait()
+    newfb_copy.wait()
 
 
 def expand(res_ref, rank_ref, newfb_ref, outer_ref, newfb_out_ref, res, rank, newfb, outer, sems):
@@ -350,7 +340,6 @@
 
 
 def on_device(inputs, target, weights, feedback, counts, blocks):
-    vmem = pl.BlockSpec(memory_space=pltpu.VMEM)
     hbm = pl.BlockSpec(memory_space=pl.ANY)
     sem = pltpu.SemaphoreType.DMA
     res, rank, newfb = pl.pallas_call(
@@ -360,18 +349,19 @@
             jax.ShapeDtypeStruct((512, 128), F32),
             jax.ShapeDtypeStruct((512, 512), BF16),
         ),
-        in_specs=[hbm, hbm, hbm, hbm, vmem, vmem],
+        in_specs=[hbm] * 6,
         out_specs=(hbm, hbm, hbm),
         scratch_shapes=[
             pltpu.VMEM((4, 512, 512), BF16),
             pltpu.VMEM((4, 512, 512), BF16),
             pltpu.VMEM((4, 512, 512), BF16),
             pltpu.VMEM((512, 512), F32),
-            pltpu.VMEM((4, 2, 128, 256), BF16),
-            pltpu.VMEM((4, 2, 128, 256), BF16),
+            pltpu.VMEM((2, 4, 128, 256), BF16),
+            pltpu.VMEM((2, 4, 128, 256), BF16),
             pltpu.VMEM((2, 512, 256), BF16),
-            pltpu.VMEM((4, 2, 512, 256), BF16),
-            pltpu.VMEM((4, 2, 512, 256), BF16),
+            pltpu.VMEM((2, 512, 256), F32),
+            pltpu.VMEM((2, 4, 512, 256), BF16),
+            pltpu.VMEM((2, 4, 512, 256), BF16),
             pltpu.VMEM((4, 128, 128), F32),
             pltpu.VMEM((4, 128, 128), BF16),
             pltpu.VMEM((4, 128, 128), BF16),
@@ -391,20 +381,22 @@
             pltpu.VMEM((256, 128), BF16),
             pltpu.VMEM((128, 512), BF16),
             pltpu.VMEM((512, 512), BF16),
+            pltpu.VMEM((1, 128), I32),
+            pltpu.VMEM((1, 1), I32),
             pltpu.VMEM((512, 128), F32),
             pltpu.VMEM((512, 512), BF16),
-            sem((4, 4)), sem((4, 4)),
-            sem((4, 2)), sem((4, 2)),
-            sem((7,)),
-            sem((4, 2)), sem((4, 2)),
-            sem((4, 2)), sem((4, 2)),
-            sem((4, 2)), sem((4, 2)),
-            sem((4,)), sem((4,)),
-            sem((4,)), sem((4,)),
-            sem((16,)), sem((16,)),
-            sem, sem,
-            sem((16,)), sem((16,)),
-            sem((16,)), sem((16,)),
+            sem, sem((4,)),
+            sem, sem((4, 2)),
+            sem((6,)),
+            sem, sem((2,)),
+            sem, sem((2,)),
+            sem, sem((2,)),
+            sem, sem,
+            sem, sem, sem, sem,
+            sem, sem,
+            sem, sem,
+            sem, sem,
+            sem, sem,
             sem, sem,
             sem((3,)),
             pltpu.SemaphoreType.REGULAR((3,)),

time: 74.9 us -> 71.4 us (0.953)
  Pallas kernels: 72.9 us -> 70 us
    pallas_call x1, Pallas kernels: 70.2 us -> 67.3 us  [on_device(): pl.pallas_call(kernel, out_shape=(jax.ShapeDtypeStruct((512, 128), BF16),...]
where the time goes in v3:
time: 71.4 us; the launch traced here: 71.3 us
  Pallas kernels  70 us (98%)
  between operations  1.29 us (2%)
    pallas_call x1, Pallas kernels, on_device(): pl.pallas_call(kernel, out_shape=(jax.ShapeDtypeStruct((512, 128), BF16),...  67.3 us
    pallas_call x1, Pallas kernels, on_device(): pl.pallas_call(expand, out_shape=(jax.ShapeDtypeStruct((512, 512), F32),...  2.72 us

profile of v3, /device:TPU:1, one launch (start us, length us, event | category | flops | bytes accessed | tf_op | source)
XLA Modules:
  0.0 71.3 jit_solution(1425985137425302532)
XLA Ops:
  1.3 67.3 %outer_sync.1 = (bf16[512,128]{1,0:T(8,128)(2,1)}, f32[512,128]{1,0:T(8,128)}, bf16[512,512]{1,0:T(8,128)(2,1)}) custom-call(bf16[128,8192]{1,0:T(8,128)(2,1)} %bitcast.6, bf16[128,512]{1,0:T(8,128)(2,1)} %bitcast.9, bf16[512,512]{1,0:T(8,128)(2,1)} %bitcast.7, bf16[512,512]{1,0:T(8,128)(2,1)} %bitcast.8, s32[1,1]{1,0:T(1,128)S(6)} %copy.8.cnt_ref, ...), custom_call_target="tpu_custom_call" | custom-call | tf_op jit(solution)/shard_map/outer_sync/pallas_call | solution.py:345
  68.6 2.7 %expand_pool.1 = (f32[512,512]{1,0:T(8,128)}, bf16[512,512]{1,0:T(8,128)(2,1)}) custom-call(bf16[512,128]{1,0:T(8,128)(2,1)} %get-tuple-element.7.res_ref, f32[512,128]{1,0:T(8,128)} %get-tuple-element.8.rank_ref, bf16[512,512]{1,0:T(8,128)(2,1)} %get-tuple-element.9.newfb_ref), custom_call_target="tpu_custom_call" | custom-call | tf_op jit(solution)/shard_map/expand_pool/pallas_call | solution.py:409

commit v4 on v3

--- a/solution.py
+++ b/solution.py
@@ -310,38 +310,29 @@
     newfb_copy.wait()
 
 
-def expand(res_ref, rank_ref, newfb_ref, outer_ref, newfb_out_ref, res, rank, newfb, outer, sems):
-    res_copy = pltpu.make_async_copy(res_ref, res, sems.at[0])
-    rank_copy = pltpu.make_async_copy(rank_ref, rank, sems.at[1])
-    newfb_copy = pltpu.make_async_copy(newfb_ref, newfb, sems.at[2])
-    newfb_out_copy = pltpu.make_async_copy(newfb, newfb_out_ref, sems.at[7])
-    rank_copy.start()
-    res_copy.start()
+def expand(res, rank, newfb, outer_ref, newfb_out_ref, outer, sems):
+    newfb_copy = pltpu.make_async_copy(newfb, newfb_out_ref, sems.at[4])
     newfb_copy.start()
-    rank_copy.wait()
-    res_copy.wait()
     places = lax.broadcasted_iota(I32, (128, 512), 1).astype(F32)
     copies = []
     for r in range(4):
         rows = slice(r * 128, (r + 1) * 128)
-        if r == 1:
-            newfb_copy.wait()
-            newfb_out_copy.start()
         for c in range(4):
             one_hot = jnp.where(rank[rows, c:c + 1] == places, 1.0, 0.0).astype(BF16)
             outer[rows, c * 128:(c + 1) * 128] = dot(one_hot, res[...])
         copies.append(pltpu.make_async_copy(
-            outer.at[pl.ds(r * 128, 128)], outer_ref.at[pl.ds(r * 128, 128)], sems.at[3 + r]
+            outer.at[pl.ds(r * 128, 128)], outer_ref.at[pl.ds(r * 128, 128)], sems.at[r]
         ))
         copies[r].start()
     for copy in copies:
         copy.wait()
-    newfb_out_copy.wait()
+    newfb_copy.wait()
 
 
 def on_device(inputs, target, weights, feedback, counts, blocks):
     hbm = pl.BlockSpec(memory_space=pl.ANY)
     sem = pltpu.SemaphoreType.DMA
+    operands = (inputs[0], target[0], weights[0], feedback[0], counts, blocks[0])
     res, rank, newfb = pl.pallas_call(
         kernel,
         out_shape=(
@@ -402,22 +393,19 @@
             pltpu.SemaphoreType.REGULAR((3,)),
         ],
         compiler_params=pltpu.CompilerParams(
-            collective_id=0, has_side_effects=True, vmem_limit_bytes=56 * 2**20
+            collective_id=0, has_side_effects=True, vmem_limit_bytes=40 * 2**20
         ),
         name="outer_sync",
-    )(inputs[0], target[0], weights[0], feedback[0], counts, blocks[0])
+    )(*[v if v.size == 1 else pltpu.with_memory_space_constraint(v, pltpu.HBM) for v in operands])
     outer, newfb = pl.pallas_call(
         expand,
         out_shape=(jax.ShapeDtypeStruct((512, 512), F32), jax.ShapeDtypeStruct((512, 512), BF16)),
-        in_specs=[hbm, hbm, hbm],
+        in_specs=[pl.BlockSpec(memory_space=pltpu.VMEM)] * 3,
         out_specs=(hbm, hbm),
-        scratch_shapes=[
-            pltpu.VMEM((512, 128), BF16), pltpu.VMEM((512, 128), F32), pltpu.VMEM((512, 512), BF16),
-            pltpu.VMEM((512, 512), F32), sem((8,)),
-        ],
-        compiler_params=pltpu.CompilerParams(vmem_limit_bytes=56 * 2**20),
+        scratch_shapes=[pltpu.VMEM((512, 512), F32), sem((5,))],
+        compiler_params=pltpu.CompilerParams(vmem_limit_bytes=8 * 2**20),
         name="expand_pool",
-    )(res, rank, newfb)
+    )(*[pltpu.with_memory_space_constraint(v, pltpu.VMEM) for v in (res, rank, newfb)])
     return outer, newfb[None]
 
 

time: 71.4 us -> 69.9 us (0.979)
  Pallas kernels: 70 us -> 68.4 us
    pallas_call x1, Pallas kernels: 2.72 us -> 1.51 us  [on_device(): pl.pallas_call(expand, out_shape=(jax.ShapeDtypeStruct((512, 512), F32),...]
where the time goes in v4:
time: 69.9 us; the launch traced here: 69.7 us
  Pallas kernels  68.4 us (98%)
  between operations  1.29 us (2%)
    pallas_call x1, Pallas kernels, on_device(): pl.pallas_call(kernel, out_shape=(jax.ShapeDtypeStruct((512, 128), BF16),...  66.9 us
    pallas_call x1, Pallas kernels, on_device(): pl.pallas_call(expand, out_shape=(jax.ShapeDtypeStruct((512, 512), F32),...  1.51 us

profile of v4, /device:TPU:1, one launch (start us, length us, event | category | flops | bytes accessed | tf_op | source)
XLA Modules:
  0.0 69.7 jit_solution(4311201935142067341)
XLA Ops:
  1.3 66.9 %outer_sync.1 = (bf16[512,128]{1,0:T(8,128)(2,1)S(1)}, f32[512,128]{1,0:T(8,128)S(1)}, bf16[512,512]{1,0:T(8,128)(2,1)S(1)}) custom-call(bf16[128,8192]{1,0:T(8,128)(2,1)} %bitcast.6, bf16[128,512]{1,0:T(8,128)(2,1)} %bitcast.9, bf16[512,512]{1,0:T(8,128)(2,1)} %bitcast.7, bf16[512,512]{1,0:T(8,128)(2,1)} %bitcast.8, s32[1,1]{1,0:T(1,128)S(6)} %copy.8.cnt_ref, ...), custom_call_target="tpu_custom_call" | custom-call | tf_op jit(solution)/shard_map/outer_sync/pallas_call | solution.py:336
  68.2 1.5 %expand_pool.1 = (f32[512,512]{1,0:T(8,128)}, bf16[512,512]{1,0:T(8,128)(2,1)}) custom-call(bf16[512,128]{1,0:T(8,128)(2,1)S(1)} %get-tuple-element.7.res, f32[512,128]{1,0:T(8,128)S(1)} %get-tuple-element.8.rank, bf16[512,512]{1,0:T(8,128)(2,1)S(1)} %get-tuple-element.9.newfb), custom_call_target="tpu_custom_call" | custom-call | tf_op jit(solution)/shard_map/expand_pool/pallas_call | solution.py:400

commit v5 on v4

--- a/solution.py
+++ b/solution.py
@@ -24,7 +24,7 @@
     res_ref, rank_ref, newfb_ref,
     xs, xt, wg, acc, kp_out, kp_in, slopes, g_own, g_out, g_in, k_acc, k_out, k_in,
     meta, meta_b, meta_z, row_sel, col_of, x_sel, k_fb, pool, kept, pool_val, pool_in, part16, rs_in, res,
-    tgt, fb, slot, cnt, rank_out, newfb,
+    tgt, fb, slot, cnt,
     x_send, x_recv, w_send, w_recv, loc_sem, kp_send, kp_recv, sl_send, sl_recv,
     g_send, g_recv, k_send, k_recv, m_send, m_recv, mt_send, mt_recv, mz_send, mz_recv,
     p_send, p_recv, rs_send, rs_recv, ag_send, ag_recv, q_send, q_recv, out_sem, z_sem,
@@ -178,13 +178,16 @@
     present = lax.fori_loop(0, 8, count, jnp.zeros((512, 128), F32)) > 0.5
     arrived(wg.at[2], w_recv.at[2, 0])
     arrived(xs.at[2, pl.ds(128, 384)], x_recv.at[2])
-    for q in range(2):
-        cols = slice(q * 256, (q + 1) * 256)
+    @pl.loop(0, 2)
+    def _(q):
+        cols = pl.ds(pl.multiple_of(q * 256, 256), 256)
         part = acc[:, cols] + dot(xs[2], wg[2, :, cols])
         acc[0:128, cols] = part[0:128, :]
-        for k in FAR_FIRST:
-            kp_out[q, k] = part[k * 128:(k + 1) * 128, :].astype(BF16)
-            remote(kp_out.at[q, k], kp_in.at[q, 4 - k], kp_send, kp_recv.at[q], along_a(k)).start()
+        for h in range(2):
+            p = 2 * q + h
+            for k in FAR_FIRST:
+                kp_out[p, k] = part[k * 128:(k + 1) * 128, h * 128:(h + 1) * 128].astype(BF16)
+                remote(kp_out.at[p, k], kp_in.at[p, 4 - k], kp_send, kp_recv.at[p], along_a(k)).start()
     prepare(2)
 
     lower = jnp.where(
@@ -197,9 +200,7 @@
     for c in range(3):
         offset = offset + jnp.where(lane > c, totals[:, c:c + 1], 0.0)
     rank = jnp.where(present, upto - 1.0 + offset, -1.0)
-    rank_out[...] = rank
-    rank_copy = pltpu.make_async_copy(rank_out, rank_ref, out_sem.at[0])
-    rank_copy.start()
+    rank_ref[...] = rank
     turned_rank = jnp.transpose(rank)[0:16, :]
     high = jnp.floor(turned_rank * (1.0 / 16.0))
     low = turned_rank - high * 16.0
@@ -209,33 +210,38 @@
     own_rank = jnp.where(own_list < UNUSED, own_rank, -1.0)
     pool[...] = jnp.where(rows512.astype(F32) == own_rank, 1.0, 0.0).astype(BF16)
 
-    for q in range(2):
-        cols = slice(q * 256, (q + 1) * 256)
-        arrived(kp_in.at[q, pl.ds(1, 3)], kp_recv.at[q])
+    for p in range(4):
+        cols, lanes = slice(p * 128, (p + 1) * 128), pl.ds(p % 2 * 128, 128)
+        arrived(kp_in.at[p, pl.ds(1, 3)], kp_recv.at[p])
         key_proj = acc[0:128, cols]
         for k in (1, 2, 3):
-            key_proj = key_proj + kp_in[q, k].astype(F32)
-        slopes[q, 0:128, :] = ((key_proj - tgt[:, cols].astype(F32)) * (1.0 / 128.0)).astype(BF16)
+            key_proj = key_proj + kp_in[p, k].astype(F32)
+        slopes[p // 2, 0:128, lanes] = ((key_proj - tgt[:, cols].astype(F32)) * (1.0 / 128.0)).astype(BF16)
         for k in FAR_FIRST:
             remote(
-                slopes.at[q, pl.ds(0, 128)], slopes.at[q, pl.ds((4 - k) * 128, 128)], sl_send, sl_recv.at[q], along_a(k)
+                slopes.at[p // 2, pl.ds(0, 128), lanes], slopes.at[p // 2, pl.ds((4 - k) * 128, 128), lanes],
+                sl_send, sl_recv.at[p], along_a(k),
             ).start()
 
-    for q in range(2):
-        arrived(slopes.at[q, pl.ds(128, 384)], sl_recv.at[q])
+    k_acc[...] = jnp.zeros_like(k_acc)
+    k_acc[0] = k_fb[...]
+
+    @pl.loop(0, 2)
+    def _(q):
+        for h in range(2):
+            arrived(slopes.at[q, pl.ds(128, 384), pl.ds(h * 128, 128)], sl_recv.at[2 * q + h])
         part = dot(x_sel[...], slopes[q])
-        for j in (2, 1, 3, 0):
-            blocks = pick(j, part[j * 128:(j + 1) * 128, :], (2 * q, 2 * q + 1))
-            if q == 0:
-                k_acc[j] = blocks
-            elif j == 0:
-                k_acc[0] = k_acc[0] + blocks + k_fb[...]
-            else:
-                k_out[j] = (k_acc[j] + blocks).astype(BF16)
-                remote(k_out.at[j], k_in.at[4 - j], k_send, k_recv, along_b(j)).start()
-    for q in range(2):
-        for j in FAR_FIRST:
-            g_out[q, j] = dot(xt[j], slopes[q]).astype(BF16)
+        for j in range(4):
+            k_acc[j] += pick(j, part[j * 128:(j + 1) * 128, :], (2 * q, 2 * q + 1))
+
+    for j in FAR_FIRST:
+        k_out[j] = k_acc[j].astype(BF16)
+        remote(k_out.at[j], k_in.at[4 - j], k_send, k_recv, along_b(j)).start()
+
+    @pl.loop(0, 6)
+    def _(i):
+        q, j = i // 3, lax.rem(i, 3) + 1
+        g_out[q, j] = dot(xt[j], slopes[q]).astype(BF16)
 
     arrived(k_in.at[pl.ds(1, 3)], k_recv)
     values = k_acc[0]
@@ -263,7 +269,8 @@
         for j in FAR_FIRST:
             remote(g_out.at[q, j], g_in.at[q, 4 - j], g_send, g_recv.at[q], along_b(j)).start()
 
-    for q in range(2):
+    @pl.loop(0, 2)
+    def _(q):
         g_own[q] = dot(xt[0], slopes[q])
 
     arrived(rs_in.at[pl.ds(1, 15)], rs_recv)
@@ -281,18 +288,17 @@
     arrived(res.at[pl.ds(0, 240)], ag_recv)
     q_copy = remote(res, res_ref.at[pl.ds(mine, 256)], q_send, q_recv, twin)
     q_copy.start()
-    res_copy = pltpu.make_async_copy(res, res_ref.at[pl.ds(mine, 256)], out_sem.at[2])
+    res_copy = pltpu.make_async_copy(res, res_ref.at[pl.ds(mine, 256)], out_sem.at[0])
     res_copy.start()
 
-    for q in range(2):
-        cols = slice(q * 256, (q + 1) * 256)
+    @pl.loop(0, 2)
+    def _(q):
+        cols = pl.ds(pl.multiple_of(q * 256, 256), 256)
         whole = g_own[q] + fb[:, cols].astype(F32)
         arrived(g_in.at[q, pl.ds(1, 3)], g_recv.at[q])
         for j in (1, 2, 3):
             whole = whole + g_in[q, j].astype(F32)
-        newfb[:, cols] = jnp.where(kept[:, cols].astype(F32) > 0.5, 0.0, whole).astype(BF16)
-    newfb_copy = pltpu.make_async_copy(newfb, newfb_ref, out_sem.at[1])
-    newfb_copy.start()
+        newfb_ref[:, cols] = jnp.where(kept[:, cols].astype(F32) > 0.5, 0.0, whole).astype(BF16)
     sent(xs.at[pl.ds(0, 3)], x_send)
     sent(wg.at[pl.ds(0, 3)], w_send)
     sent(meta_b.at[pl.ds(1, 3)], m_send)
@@ -304,10 +310,8 @@
     sent(rs_in.at[pl.ds(1, 15)], rs_send)
     sent(res.at[pl.ds(0, 240)], ag_send)
     p_copy.wait_send()
-    rank_copy.wait()
     res_copy.wait()
     q_copy.wait()
-    newfb_copy.wait()
 
 
 def expand(res, rank, newfb, outer_ref, newfb_out_ref, outer, sems):
@@ -336,19 +340,19 @@
     res, rank, newfb = pl.pallas_call(
         kernel,
         out_shape=(
-            jax.ShapeDtypeStruct((512, 128), BF16),
-            jax.ShapeDtypeStruct((512, 128), F32),
-            jax.ShapeDtypeStruct((512, 512), BF16),
+            pltpu.VMEM((512, 128), BF16),
+            pltpu.VMEM((512, 128), F32),
+            pltpu.VMEM((512, 512), BF16),
         ),
         in_specs=[hbm] * 6,
-        out_specs=(hbm, hbm, hbm),
+        out_specs=(pl.BlockSpec(memory_space=pltpu.VMEM),) * 3,
         scratch_shapes=[
             pltpu.VMEM((4, 512, 512), BF16),
             pltpu.VMEM((4, 512, 512), BF16),
             pltpu.VMEM((4, 512, 512), BF16),
             pltpu.VMEM((512, 512), F32),
-            pltpu.VMEM((2, 4, 128, 256), BF16),
-            pltpu.VMEM((2, 4, 128, 256), BF16),
+            pltpu.VMEM((4, 4, 128, 128), BF16),
+            pltpu.VMEM((4, 4, 128, 128), BF16),
             pltpu.VMEM((2, 512, 256), BF16),
             pltpu.VMEM((2, 512, 256), F32),
             pltpu.VMEM((2, 4, 512, 256), BF16),
@@ -374,14 +378,12 @@
             pltpu.VMEM((512, 512), BF16),
             pltpu.VMEM((1, 128), I32),
             pltpu.VMEM((1, 1), I32),
-            pltpu.VMEM((512, 128), F32),
-            pltpu.VMEM((512, 512), BF16),
             sem, sem((4,)),
             sem, sem((4, 2)),
             sem((6,)),
+            sem, sem((4,)),
+            sem, sem((4,)),
             sem, sem((2,)),
-            sem, sem((2,)),
-            sem, sem((2,)),
             sem, sem,
             sem, sem, sem, sem,
             sem, sem,
@@ -389,7 +391,7 @@
             sem, sem,
             sem, sem,
             sem, sem,
-            sem((3,)),
+            sem((1,)),
             pltpu.SemaphoreType.REGULAR((3,)),
         ],
         compiler_params=pltpu.CompilerParams(

time: 69.9 us -> 70.3 us (level)
  no operation moved by 1% of the time
where the time goes in v5:
time: 70.3 us; the launch traced here: 70.2 us
  Pallas kernels  68.9 us (98%)
  between operations  1.29 us (2%)
    pallas_call x1, Pallas kernels, on_device(): pl.pallas_call(kernel, out_shape=(pltpu.VMEM((512, 128), BF16), pltpu.VME...  67.4 us
    pallas_call x1, Pallas kernels, on_device(): pl.pallas_call(expand, out_shape=(jax.ShapeDtypeStruct((512, 512), F32),...  1.51 us

profile of v5, /device:TPU:1, one launch (start us, length us, event | category | flops | bytes accessed | tf_op | source)
XLA Modules:
  0.0 70.2 jit_solution(8532623320995024739)
XLA Ops:
  1.3 67.4 %outer_sync.1 = (bf16[512,128]{1,0:T(8,128)(2,1)S(1)}, f32[512,128]{1,0:T(8,128)S(1)}, bf16[512,512]{1,0:T(8,128)(2,1)S(1)}) custom-call(bf16[128,8192]{1,0:T(8,128)(2,1)} %bitcast.6, bf16[128,512]{1,0:T(8,128)(2,1)} %bitcast.9, bf16[512,512]{1,0:T(8,128)(2,1)} %bitcast.7, bf16[512,512]{1,0:T(8,128)(2,1)} %bitcast.8, s32[1,1]{1,0:T(1,128)S(6)} %copy.8.cnt_ref, ...), custom_call_target="tpu_custom_call" | custom-call | tf_op jit(solution)/shard_map/outer_sync/pallas_call | solution.py:340
  68.7 1.5 %expand_pool.1 = (f32[512,512]{1,0:T(8,128)}, bf16[512,512]{1,0:T(8,128)(2,1)}) custom-call(bf16[512,128]{1,0:T(8,128)(2,1)S(1)} %get-tuple-element.7.res, f32[512,128]{1,0:T(8,128)S(1)} %get-tuple-element.8.rank, bf16[512,512]{1,0:T(8,128)(2,1)S(1)} %get-tuple-element.9.newfb), custom_call_target="tpu_custom_call" | custom-call | tf_op jit(solution)/shard_map/expand_pool/pallas_call | solution.py:402
